TPU v7x, 512 devices: a whole 4x8x8 slice. The times are simulated.
512 devices in a mesh: tok: 32 (over y_hi, z), head: 16 (over x, y_lo, core).
Axes of the slice: x: 4, y: 8 (y_hi: 4, y_lo: 2; y = y_hi * 2 + y_lo), z: 8, core: 2. Of those that a mesh axis runs over, the one named last changes fastest.
Arguments:
- queries: bfloat16 [1024, 12288], P('head', 'tok'), may hold values from -8 to 8
- keys: bfloat16 [1024, 12288], P('head', 'tok'), may hold values from -8 to 8
- values: bfloat16 [1024, 12288], P('head', 'tok'), may hold values from -6 to 6
- out_grad: bfloat16 [1024, 12288], P('head', 'tok'), may hold values from -6 to 6
- w_out: bfloat16 [1024, 1024], P('head'), may hold values from -0.1875 to 0.1875
- counts: int32 [32], P('tok'), may hold values from 48 to 384, as said below
- keep: int32 [12288], P('tok'), may hold values 0 or 1
Outputs:
- dq: bfloat16 [1024, 12288], P('head', 'tok')
- dk: bfloat16 [1024, 12288], P('head', 'tok')
- dv: bfloat16 [1024, 12288], P('head', 'tok')
- d_wout: float32 [1024, 1024], P('head')
Inputs may be any that keep to these rules, and one draw needn't show every extreme that they name: The valid tokens of a block are its first counts entries; some block is full, and some block holds exactly 48.
All inputs are finite; a program needn't handle non-finite values. No bound on the sum of `keep` on one device may be relied on, other than what follows from the above.
Results may differ from a plain program's by a relative error of at most 0.04.
Values may be sent and summed in bfloat16 or wider, within the bound.
No kernel may reach another device: no remote copies, remote signals or barrier semaphores. Data moves between devices by JAX's collectives and lax.ppermute only.
A program may use at most 64 MiB of HBM per device.

v0:
```python
import math

import jax
import jax.numpy as jnp
from jax import lax
from jax.sharding import PartitionSpec as P

HD = 64


NEGATIVE_FILL = -1e30


def split_rows(rows):
    size = rows
    while size > 1024 and size % 2 == 0:
        size = size // 2
    return (size, rows // size)


def over_blocks(update, carry, arrays):
    size, count = split_rows(arrays[0].shape[1])

    def one_block(index, state):
        offset = index * size
        sliced = tuple((lax.dynamic_slice_in_dim(item, offset, size, 1) for item in arrays))
        return update(state, sliced, offset)

    return lax.fori_loop(0, count, one_block, carry)


def on_device(queries, keys, values, out_grad, w_out, counts, keep):
    scale = 1.0 / math.sqrt(HD)
    feats, width = queries.shape
    heads = feats // HD
    pos = jnp.arange(width, dtype=jnp.int32)
    valid_entries = pos < counts[0]
    live = jnp.where(valid_entries, keep, 0).astype(jnp.bfloat16)
    grad = out_grad * live[None, :]
    key_live = valid_entries.astype(jnp.bfloat16)[None, :]
    q_heads = queries.reshape(heads, HD, width)
    k_heads = keys.reshape(heads, HD, width)
    v_heads = values.reshape(heads, HD, width)

    def forward_block(carry, blk, start):
        running_maximum, total, acc = carry
        k_part, v_part, l_part = blk
        mask = (l_part[0] > 0)[None, None, :]
        k_rows = k_part.reshape(heads, HD, -1)
        v_rows = v_part.reshape(heads, HD, -1).astype(jnp.float32)
        score_matrix = (
            jnp.einsum("hdq,hdk->hqk", q_heads, k_rows, preferred_element_type=jnp.float32) * scale
        )
        score_matrix = jnp.where(mask, score_matrix, NEGATIVE_FILL)
        new_top = jnp.maximum(running_maximum, jnp.max(score_matrix, axis=2))
        fade = jnp.exp(running_maximum - new_top)
        exponent_terms = jnp.where(mask, jnp.exp(score_matrix - new_top[:, :, None]), 0.0)
        total = total * fade + jnp.sum(exponent_terms, axis=2)
        acc = acc * fade[:, None, :] + jnp.einsum(
            "hqk,hdk->hdq",
            exponent_terms,
            v_rows,
            precision=lax.Precision.HIGHEST,
            preferred_element_type=jnp.float32,
        )
        return (new_top, total, acc)

    start_state = (
        jnp.full((heads, width), NEGATIVE_FILL, jnp.float32),
        jnp.zeros((heads, width), jnp.float32),
        jnp.zeros((heads, HD, width), jnp.float32),
    )
    running_maximum, total, acc = over_blocks(
        forward_block,
        start_state,
        (
            lax.all_gather(keys, "tok", axis=1, tiled=True),
            lax.all_gather(values, "tok", axis=1, tiled=True),
            lax.all_gather(key_live, "tok", axis=1, tiled=True),
        ),
    )
    log_sum_exponent = running_maximum + jnp.log(total)
    attn = (acc / total[:, None, :]).astype(jnp.bfloat16)
    attn_flat = attn.reshape(feats, width)
    piece = lax.all_gather(grad, "head", axis=0, tiled=True)
    rows = piece.shape[0]
    d_acc = jnp.dot(w_out, piece, preferred_element_type=jnp.float32)
    part = lax.dot_general(
        attn_flat, piece, (((1,), (1,)), ((), ())), preferred_element_type=jnp.float32
    )
    w_acc = part
    d_acc, w_acc = (d_acc, w_acc)
    weight_grad = lax.psum(w_acc, "tok")
    d_attn_flat = d_acc.astype(jnp.bfloat16)
    d_attn = d_attn_flat.reshape(heads, HD, width)
    delta = jnp.sum(d_attn.astype(jnp.float32) * attn.astype(jnp.float32), axis=1)
    own_mask = valid_entries[None, None, :]

    def query_block(dq_acc, blk, start):
        k_part, v_part, l_part = blk
        mask = (l_part[0] > 0)[None, None, :]
        k_rows = k_part.reshape(heads, HD, -1)
        v_rows = v_part.reshape(heads, HD, -1)
        score_matrix = (
            jnp.einsum("hdq,hdk->hqk", q_heads, k_rows, preferred_element_type=jnp.float32) * scale
        )
        probability_rows = jnp.where(
            mask, jnp.exp(score_matrix - log_sum_exponent[:, :, None]), 0.0
        )
        dprob = jnp.einsum("hdq,hdk->hqk", d_attn, v_rows, preferred_element_type=jnp.float32)
        dscore = probability_rows * (dprob - delta[:, :, None])
        return dq_acc + jnp.einsum(
            "hqk,hdk->hdq", dscore.astype(jnp.bfloat16), k_rows, preferred_element_type=jnp.float32
        )

    zero = jnp.zeros((heads, HD, width), jnp.float32)
    dq_acc = over_blocks(
        query_block,
        zero,
        (
            lax.all_gather(keys, "tok", axis=1, tiled=True),
            lax.all_gather(values, "tok", axis=1, tiled=True),
            lax.all_gather(key_live, "tok", axis=1, tiled=True),
        ),
    )
    lse_all, delta_all = (
        lax.all_gather(log_sum_exponent, "tok", axis=1, tiled=True),
        lax.all_gather(delta, "tok", axis=1, tiled=True),
    )

    def key_block(carry, blk, start):
        dk_acc, dv_acc = carry
        q_part, d_part = blk
        rows = q_part.shape[1]
        q_rows = q_part.reshape(heads, HD, rows)
        d_rows = d_part.reshape(heads, HD, rows)
        lse_part = lax.dynamic_slice_in_dim(lse_all, start, rows, 1)
        delta_part = lax.dynamic_slice_in_dim(delta_all, start, rows, 1)
        score_matrix = (
            jnp.einsum("hdq,hdk->hqk", q_rows, k_heads, preferred_element_type=jnp.float32) * scale
        )
        probability_rows = jnp.where(own_mask, jnp.exp(score_matrix - lse_part[:, :, None]), 0.0)
        dprob = jnp.einsum("hdq,hdk->hqk", d_rows, v_heads, preferred_element_type=jnp.float32)
        dscore = probability_rows * (dprob - delta_part[:, :, None])
        dk_acc = dk_acc + jnp.einsum(
            "hqk,hdq->hdk", dscore.astype(jnp.bfloat16), q_rows, preferred_element_type=jnp.float32
        )
        dv_acc = dv_acc + jnp.einsum(
            "hqk,hdq->hdk",
            probability_rows.astype(jnp.bfloat16),
            d_rows,
            preferred_element_type=jnp.float32,
        )
        return (dk_acc, dv_acc)

    dk_acc, dv_acc = over_blocks(
        key_block,
        (zero, zero),
        (
            lax.all_gather(queries, "tok", axis=1, tiled=True),
            lax.all_gather(d_attn_flat, "tok", axis=1, tiled=True),
        ),
    )
    dq = (scale * dq_acc).astype(jnp.bfloat16).reshape(feats, width)
    dk = (scale * dk_acc).astype(jnp.bfloat16).reshape(feats, width)
    dv = dv_acc.astype(jnp.bfloat16).reshape(feats, width)
    return (dq, dk, dv, weight_grad)


def solution(mesh):
    return jax.shard_map(
        on_device,
        mesh=mesh,
        in_specs=(
            P("head", "tok"),
            P("head", "tok"),
            P("head", "tok"),
            P("head", "tok"),
            P("head", None),
            P("tok"),
            P("tok"),
        ),
        out_specs=(P("head", "tok"), P("head", "tok"), P("head", "tok"), P("head", None)),
        check_vma=False,
    )
```

profile of v0, /device:TPU:6, one launch (start us, length us, event | category | flops | bytes accessed | tf_op | source)
XLA Modules:
  0.0 758.0 jit_solution(11936477285264853427)
XLA Ops:
  10.2 88.7 %all_gather.28 = bf16[1,12288]{1,0:T(2,128)(2,1)S(1)} all-gather(bf16[1,384]{1,0:T(2,128)(2,1)S(1)} %compare_convert_fusion), channel_id=1, replica_groups=mesh['tok'=32,'head'=16] {'tok'}, dimensions={1}, use_global_device_ids=true | all-gather | bytes 25344 | tf_op jit(solution)/shard_map/all_gather | solution.py:123
  100.4 20.1 %all_gather.30 = bf16[1024,384]{1,0:T(8,128)(2,1)S(1)} all-gather(bf16[64,384]{1,0:T(8,128)(2,1)S(1)} %broadcast_multiply_fusion), channel_id=1, replica_groups=mesh['tok'=32,'head'=16] {'head'}, dimensions={0}, use_global_device_ids=true | all-gather | bytes 835584 | tf_op jit(solution)/shard_map/all_gather | solution.py:85
  120.5 59.9 %all-gather.9.cloned.1.call-done = bf16[64,12288]{1,0:T(8,128)(2,1)} async-done(((bf16[64,384]{1,0:T(8,128)(2,1)}), bf16[64,12288]{1,0:T(8,128)(2,1)}) %all-gather.9.cloned.1.call-update) | async-done | bytes 1572880 | tf_op jit(solution)/shard_map/all_gather | solution.py:122
  180.4 53.2 %while.48 = (s32[]{:T(128)}, f32[1,384]{1,0:T(1,128)S(1)}, f32[1,384]{1,0:T(1,128)S(1)}, f32[1,64,384]{2,1,0:T(8,128)S(1)}, bf16[1,12288]{1,0:T(2,128)(2,1)S(1)}...) while((s32[]{:T(128)}, f32[1,384]{1,0:T(1,128)S(1)}, ...), condition=%wide.region_3.4_spmd.clone, body=%wide.region_0.3_spmd.clone.sunk | while | flops 266678784 | bytes 4012227 | solution.py:29
  182.0 1.7 fusion.99
  185.3 1.7 fusion.99
  188.6 1.7 fusion.99
  192.0 1.7 fusion.99
  195.3 1.7 fusion.99
  198.6 1.7 fusion.99
  201.9 1.7 fusion.99
  205.3 1.7 fusion.99
  208.6 1.7 fusion.99
  211.9 1.7 fusion.99
  215.2 1.7 fusion.99
  218.6 1.7 fusion.99
  221.9 1.7 fusion.99
  225.2 1.7 fusion.99
  228.5 1.7 fusion.99
  231.9 1.7 fusion.99
  234.6 48.0 %while.49 = (s32[]{:T(128)}, f32[1,64,384]{2,1,0:T(8,128)S(1)}, bf16[64,12288]{1,0:T(8,128)(2,1)}, bf16[1,12288]{1,0:T(2,128)(2,1)S(1)}, bf16[1,64,384]{2,1,0:T(...) while((s32[]{:T(128)}, f32[1,64,384]{2,1,0:T(8,128)S(1)}, ...), condition=%wide.region_6.7_spmd.clone, body=%wide.region_5.6_spmd.clone.sunk | while | flops 115067136 | bytes 3159792 | solution.py:29
  241.9 1.6 fusion.105
  244.9 1.6 fusion.105
  247.9 1.6 fusion.105
  256.9 1.6 fusion.105
  265.9 1.6 fusion.105
  274.9 1.6 fusion.105
  282.6 78.1 %all_gather.32 = f32[1,12288]{1,0:T(1,128)S(1)} all-gather(f32[1,384]{1,0:T(1,128)S(1)} %get-tuple-element.960), channel_id=1, replica_groups=mesh['tok'=32,'head'=16] {'tok'}, dimensions={1}, use_global_device_ids=true | all-gather | bytes 50688 | tf_op jit(solution)/shard_map/all_gather | solution.py:127
  360.7 76.8 %all-gather.1 = f32[32,1,384]{2,1,0:T(1,128)S(1)} all-gather(f32[1,1,384]{2,1,0:T(1,128)S(1)} %reshape.237), channel_id=2, replica_groups=mesh['tok'=32,'head'=16] {'tok'}, dimensions={0}, use_global_device_ids=true | all-gather | bytes 50688 | tf_op jit(solution)/shard_map/all_gather | solution.py:128
  439.3 75.7 %while.50 = (s32[]{:T(128)}, f32[1,64,384]{2,1,0:T(8,128)S(1)}, f32[1,64,384]{2,1,0:T(8,128)S(1)}, bf16[64,12288]{1,0:T(8,128)(2,1)}, bf16[1,64,384]{2,1,0:T(8,1...) while((s32[]{:T(128)}, f32[1,64,384]{2,1,0:T(8,128)S(1)}, ...), condition=%wide.region_8.9_spmd.clone, body=%wide.region_7.8_spmd.clone.sunk | while | flops 153158016 | bytes 4444629 | solution.py:29
  515.7 234.2 %all-reduce.2.cloned.1.call-done = f32[64,1024]{1,0:T(8,128)} async-done(((f32[64,1024]{1,0:T(8,128)}), f32[64,1024]{1,0:T(8,128)}) %all-reduce.2.cloned.1.call-update) | async-done | bytes 262160 | tf_op jit(solution)/shard_map/psum | solution.py:93
  749.8 1.7 copy.40
  (317 shorter events, 144.9 us)
Async XLA Ops:
  7.2 226.4 %copy-start = (bf16[64,1024]{1,0:T(8,128)(2,1)S(1)}, bf16[64,1024]{1,0:T(8,128)(2,1)}, u32[]{:S(2)}) copy-start(bf16[64,1024]{1,0:T(8,128)(2,1)} %param.17) | copy-start | bytes 393220
  7.2 113.3 %all-gather.7.cloned.1.call-start = ((), (), s32[]{:S(2)}) async-start(), calls=%async_computation | async-start | bytes 1622016 | tf_op jit(solution)/shard_map/all_gather | solution.py:121
  7.9 172.5 %all-gather.9.cloned.1.call-start = ((), (), s32[]{:S(2)}) async-start(), calls=%async_computation.1 | async-start | bytes 1622016 | tf_op jit(solution)/shard_map/all_gather | solution.py:122
  8.7 430.6 %all-gather.11.cloned.1.call-start = ((), (), s32[]{:S(2)}) async-start(), calls=%async_computation.2 | async-start | bytes 1622016 | tf_op jit(solution)/shard_map/all_gather | solution.py:160
  9.4 429.9 %all-gather.13.cloned.1.call-start = ((), (), s32[]{:S(2)}) async-start(), calls=%async_computation.3 | async-start | bytes 1622016 | tf_op jit(solution)/shard_map/all_gather | solution.py:161
  234.5 515.3 %all-reduce.2.cloned.1.call-start = ((), (), s32[]{:S(2)}) async-start(), calls=%async_computation.4 | async-start | bytes 524288 | tf_op jit(solution)/shard_map/psum | solution.py:93
  234.6 1.3 copy-start.1
  237.6 1.3 copy-start.1
  240.6 1.4 copy-start.1
  243.6 1.3 copy-start.1
  246.6 1.3 copy-start.1
  249.6 1.3 copy-start.1
  252.6 1.3 copy-start.1
  255.6 1.3 copy-start.1
  258.6 1.3 copy-start.1
  261.6 1.3 copy-start.1
  264.6 1.3 copy-start.1
  267.6 1.3 copy-start.1
  270.6 1.3 copy-start.1
  273.6 1.3 copy-start.1
  276.6 1.3 copy-start.1
  279.6 1.3 copy-start.1
  282.6 156.7 %copy-start.2 = (bf16[64,384]{1,0:T(8,128)(2,1)S(1)}, bf16[64,384]{1,0:T(8,128)(2,1)}, u32[]{:S(2)}) copy-start(bf16[64,384]{1,0:T(8,128)(2,1)} %param.15) | copy-start | bytes 147460
  282.6 156.7 %copy-start.3 = (bf16[64,384]{1,0:T(8,128)(2,1)S(1)}, bf16[64,384]{1,0:T(8,128)(2,1)}, u32[]{:S(2)}) copy-start(bf16[64,384]{1,0:T(8,128)(2,1)} %param.14) | copy-start | bytes 147460
Sparse Core Ops, SparseCore 0:
  11.1 87.2 all-gather.6
  101.5 78.8 all-gather.8
  183.5 77.5 all-gather.10
  264.6 78.3 all-gather.12
  439.3 310.4 all-reduce.1
where the time goes:
time: 762 us; the launch traced here: 758 us
  waiting for transfers between devices  296 us (39%)
  blocking collectives  264 us (35%)
  matrix products  159 us (21%)
  other arithmetic  19.7 us (3%)
  between operations  14.6 us (2%)
    psum x1, waiting for transfers between devices, on_device(): weight_grad = lax.psum(w_acc, 'tok')  234 us
    all_gather x1, blocking collectives, on_device(): lax.all_gather(key_live, 'tok', axis=1, tiled=True)  88.7 us
    all_gather x1, blocking collectives, on_device(): lax.all_gather(log_sum_exponent, 'tok', axis=1, tiled=True)  78.1 us
    all_gather x1, blocking collectives, on_device(): lax.all_gather(delta, 'tok', axis=1, tiled=True)  76.8 us
    all_gather x1, waiting for transfers between devices, on_device(): lax.all_gather(values, 'tok', axis=1, tiled=True)  59.9 us
    dot_general x16, matrix products, forward_block(): jnp.einsum('hqk,hdk->hdq', exponent_terms, v_rows, precision=lax.Precisio...  27 us
    dot_general x16, matrix products, query_block(): jnp.einsum('hqk,hdk->hdq', dscore.astype(jnp.bfloat16), k_rows, preferred...  25.9 us
    dot_general x16, matrix products, key_block(): jnp.einsum('hqk,hdq->hdk', dscore.astype(jnp.bfloat16), q_rows, preferred...  24.6 us
  transfers between devices with their start and end apart: 5, of which 2 were waited for; matrix products, arithmetic and copies ran while one was open for 24% of the time, Pallas kernels for 0%

commit v1 on v0

v1 whole, which is shorter than its diff:
```python
import jax
import jax.numpy as jnp
from jax import lax
from jax.experimental import pallas as pl
from jax.experimental.pallas import tpu as pltpu
from jax.sharding import PartitionSpec as P

HD = 64
TB = 384
NY = 4
NZ = 8
CH = 128
NCH = TB // CH
TK = 256
TQ = 256
KROWS = NZ * TB
QCOLS = NY * TB
EXT = 16
BIAS = -30000.0
BF = jnp.bfloat16
F32 = jnp.float32
Z_GROUPS = [[y * NZ + z for z in range(NZ)] for y in range(NY)]
Y_GROUPS = [[y * NZ + z for y in range(NY)] for z in range(NZ)]


def dot(a, b):
    return jnp.dot(a, b, preferred_element_type=F32)


def dot_nt(a, b):
    return lax.dot_general(a, b, (((1,), (1,)), ((), ())), preferred_element_type=F32)


def pieces(x):
    hi = x.astype(BF)
    rest = x - hi.astype(F32)
    mid = rest.astype(BF)
    low = (rest - mid.astype(F32)).astype(BF)
    return hi, mid, low


def count_of(meta):
    meta = meta.astype(F32)
    return jnp.max(meta[0:1, 0:CH] * 16.0 + meta[1:2, 0:CH]).astype(jnp.int32)


def pack_keys(kv_ref, kvp_ref):
    lane = lax.broadcasted_iota(jnp.int32, (TB, CH), 1)
    row = lax.broadcasted_iota(jnp.int32, (TB, CH), 0)
    ones = jnp.where((lane >= 1) & (lane <= 3), 1.0, 0.0)
    offset = jnp.int32(0)
    offsets = []
    for b in range(NZ):
        cnt = count_of(kv_ref[b, TB : TB + EXT, :])
        here = pl.multiple_of(offset, 16)
        kvp_ref[pl.ds(here, TB), 0:CH] = kv_ref[b, 0:TB, :]
        aux = jnp.where((lane == 0) & (row >= cnt), BIAS, ones)
        kvp_ref[pl.ds(here, TB), CH : 2 * CH] = aux.astype(BF)
        size = ((cnt + 15) // 16) * 16
        offsets.append((here, size))
        offset = offset + size
    here = pl.multiple_of(offset, 16)
    kvp_ref[pl.ds(here, TK), 0:CH] = jnp.zeros((TK, CH), BF)
    tail = jnp.where(lane[0:TK] == 0, BIAS, ones[0:TK])
    kvp_ref[pl.ds(here, TK), CH : 2 * CH] = tail.astype(BF)
    return offsets, (offset + TK - 1) // TK


def eye(n):
    r = lax.broadcasted_iota(jnp.int32, (n, n), 0)
    c = lax.broadcasted_iota(jnp.int32, (n, n), 1)
    return jnp.where(r == c, 1.0, 0.0).astype(BF)


def transpose_keys(kvp_ref, kvt_ref, n_key_tiles):
    unit = eye(CH)

    def one(kt, _):
        at = pl.multiple_of(kt * TK, TK)
        kvt_ref[:, pl.ds(at, TK)] = dot_nt(unit, kvp_ref[pl.ds(at, TK), 0:CH]).astype(BF)
        return 0

    lax.fori_loop(0, n_key_tiles, one, 0)


def query_chunks(x_ref):
    n = jnp.int32(0)
    chunks = []
    for b in range(NY):
        cnt = count_of(x_ref[b, 2 * HD : 2 * HD + EXT, :])
        for c in range(NCH):
            active = cnt > c * CH
            chunks.append((b, c, active, pl.multiple_of(n * CH, CH)))
            n = n + active.astype(jnp.int32)
    return chunks, (n * CH + TQ - 1) // TQ


def pack_queries(x_ref, ws_ref, wd_ref, chunks):
    ws_ref[...] = jnp.zeros(ws_ref.shape, BF)
    wd_ref[...] = jnp.zeros(wd_ref.shape, BF)
    first = lax.broadcasted_iota(jnp.int32, (EXT, QCOLS + CH), 0) == 0
    ws_ref[CH : CH + EXT, :] = jnp.where(first, 1.0, 0.0).astype(BF)
    for b, c, active, at in chunks:
        @pl.when(active)
        def _():
            part = slice(c * CH, (c + 1) * CH)
            ws_ref[0:HD, pl.ds(at, CH)] = x_ref[b, 0:HD, part]
            wd_ref[HD : 2 * HD, pl.ds(at, CH)] = x_ref[b, HD : 2 * HD, part]


def forward_kernel(kv_ref, x_ref, out_ref, kvp_ref, kvt_ref, ws_ref, wd_ref, acc_ref, st_ref, stu_ref):
    _, n_key_tiles = pack_keys(kv_ref, kvp_ref)
    transpose_keys(kvp_ref, kvt_ref, n_key_tiles)
    chunks, n_query_tiles = query_chunks(x_ref)
    pack_queries(x_ref, ws_ref, wd_ref, chunks)

    def query_tile(qt, _):
        q0 = pl.multiple_of(qt * TQ, TQ)
        ws = ws_ref[:, pl.ds(q0, TQ)]
        wd = wd_ref[:, pl.ds(q0, TQ)]

        def key_tile(kt, carry):
            top, total, dsum, acc = carry
            k0 = pl.multiple_of(kt * TK, TK)
            kv = kvp_ref[pl.ds(k0, TK), :]
            s = dot(kv, ws)
            dp = dot(kv, wd)
            new = jnp.maximum(top, jnp.max(s, axis=0, keepdims=True))
            e = jnp.exp(s - new)
            fade = jnp.exp(top - new)
            total = total * fade + jnp.sum(e, axis=0, keepdims=True)
            dsum = dsum * fade + jnp.sum(e * dp, axis=0, keepdims=True)
            acc = acc * fade + dot(kvt_ref[HD : 2 * HD, pl.ds(k0, TK)], e.astype(BF))
            return new, total, dsum, acc

        zero = jnp.zeros((1, TQ), F32)
        top, total, dsum, acc = lax.fori_loop(
            0, n_key_tiles, key_tile, (zero - 1e30, zero, zero, jnp.zeros((HD, TQ), F32))
        )
        acc_ref[:, pl.ds(q0, TQ)] = acc / total
        st_ref[0:1, pl.ds(q0, TQ)] = top
        st_ref[1:2, pl.ds(q0, TQ)] = total
        st_ref[2:3, pl.ds(q0, TQ)] = dsum
        return 0

    lax.fori_loop(0, n_query_tiles, query_tile, 0)

    row = lax.broadcasted_iota(jnp.int32, (EXT, TB), 0)
    stu_ref[...] = jnp.where((row >= NY) & (row < 2 * NY), 1.0, 0.0)
    out_ref[...] = jnp.zeros(out_ref.shape, BF)
    for b, c, active, at in chunks:
        @pl.when(active)
        def _():
            part = slice(c * CH, (c + 1) * CH)
            out_ref[b, 0:HD, part] = acc_ref[:, pl.ds(at, CH)].astype(BF)
            for i in range(3):
                stu_ref[i * NY + b : i * NY + b + 1, part] = st_ref[i : i + 1, pl.ds(at, CH)]
    split = pieces(stu_ref[...])
    for b in range(NY):
        for i in range(3):
            out_ref[b, HD + i * EXT : HD + (i + 1) * EXT, :] = split[i]


def merged_stats(r_ref):
    stats = []
    for s in range(NY):
        st = r_ref[s, HD : HD + EXT, :].astype(F32)
        st = st + r_ref[s, HD + EXT : HD + 2 * EXT, :].astype(F32)
        stats.append(st + r_ref[s, HD + 2 * EXT : HD + 3 * EXT, :].astype(F32))
    top = stats[0][0:NY]
    for s in range(1, NY):
        top = jnp.maximum(top, stats[s][0:NY])
    shares = []
    total = jnp.zeros((NY, TB), F32)
    dsum = jnp.zeros((NY, TB), F32)
    for s in range(NY):
        fade = jnp.exp(stats[s][0:NY] - top)
        shares.append(stats[s][NY : 2 * NY] * fade)
        total = total + shares[s]
        dsum = dsum + stats[s][2 * NY : 3 * NY] * fade
    return top + jnp.log(total), dsum / total, [share / total for share in shares]


def combine_kernel(y_ref, r_ref, grad_ref, out_ref, share_ref):
    _, _, shares = merged_stats(r_ref)
    for s in range(NY):
        share_ref[s] = shares[s]
    own = y_ref[0]
    attn = jnp.zeros((HD, TB), F32)
    for s in range(NY):
        attn = attn + r_ref[s, 0:HD, :].astype(F32) * share_ref[s, pl.ds(own, 1), :]
    attn = attn.astype(BF)
    for z in range(NZ):
        part = dot_nt(attn, grad_ref[z * CH : (z + 1) * CH, :])
        for y in range(NY):
            out_ref[y * NZ + z] = part[y * 16 : (y + 1) * 16, :].astype(BF)


def backward_kernel(
    kv_ref, x_ref, r_ref, dq_ref, dkv_ref, kvp_ref, kvt_ref, ws_ref, wd_ref, xq_ref, xd_ref, lse_ref, dl_ref, dqa_ref, dkva_ref
):
    offsets, n_key_tiles = pack_keys(kv_ref, kvp_ref)
    transpose_keys(kvp_ref, kvt_ref, n_key_tiles)
    chunks, n_query_tiles = query_chunks(x_ref)
    pack_queries(x_ref, ws_ref, wd_ref, chunks)
    lse, delta, _ = merged_stats(r_ref)
    for i, piece in enumerate(pieces(-lse)):
        lse_ref[i] = piece.astype(F32)
    for i, piece in enumerate(pieces(-delta)):
        dl_ref[i] = piece.astype(F32)
    row = lax.broadcasted_iota(jnp.int32, (EXT, CH), 0)
    for b, c, active, at in chunks:
        @pl.when(active)
        def _():
            part = slice(c * CH, (c + 1) * CH)
            tile_s = jnp.where(row == 0, 1.0, 0.0)
            tile_d = jnp.zeros((EXT, CH), F32)
            for i in range(3):
                tile_s = jnp.where(row == i + 1, lse_ref[i, b : b + 1, part], tile_s)
                tile_d = jnp.where(row == i + 1, dl_ref[i, b : b + 1, part], tile_d)
            ws_ref[CH : CH + EXT, pl.ds(at, CH)] = tile_s.astype(BF)
            wd_ref[CH : CH + EXT, pl.ds(at, CH)] = tile_d.astype(BF)

    unit = eye(TQ)

    def turn(qt, _):
        q0 = pl.multiple_of(qt * TQ, TQ)
        xq_ref[pl.ds(q0, TQ), :] = dot_nt(unit, ws_ref[0:CH, pl.ds(q0, TQ)]).astype(BF)
        xd_ref[pl.ds(q0, TQ), :] = dot_nt(unit, wd_ref[0:CH, pl.ds(q0, TQ)]).astype(BF)
        return 0

    lax.fori_loop(0, n_query_tiles, turn, 0)
    dqa_ref[...] = jnp.zeros(dqa_ref.shape, F32)

    def key_tile(kt, _):
        k0 = pl.multiple_of(kt * TK, TK)
        kv = kvp_ref[pl.ds(k0, TK), :]
        kt_rows = kvt_ref[0:HD, pl.ds(k0, TK)]

        def query_tile(qt, acc):
            q0 = pl.multiple_of(qt * TQ, TQ)
            prob = jnp.exp(dot(kv, ws_ref[:, pl.ds(q0, TQ)]))
            dscore = (prob * dot(kv, wd_ref[:, pl.ds(q0, TQ)])).astype(BF)
            prob = prob.astype(BF)
            dqa_ref[:, pl.ds(q0, TQ)] += dot(kt_rows, dscore)
            acc = acc + dot(dscore, xq_ref[pl.ds(q0, TQ), :])
            return acc + dot(prob, xd_ref[pl.ds(q0, TQ), :])

        dkva_ref[pl.ds(k0, TK), :] = lax.fori_loop(0, n_query_tiles, query_tile, jnp.zeros((TK, CH), F32))
        return 0

    lax.fori_loop(0, n_key_tiles, key_tile, 0)

    dq_ref[...] = jnp.zeros(dq_ref.shape, BF)
    for b, c, active, at in chunks:
        @pl.when(active)
        def _():
            dq_ref[b, c * HD : (c + 1) * HD, :] = (0.125 * dqa_ref[:, pl.ds(at, CH)]).astype(BF)
    krow = lax.broadcasted_iota(jnp.int32, (TB, CH), 0)
    for b in range(NZ):
        here, size = offsets[b]
        got = dkva_ref[pl.ds(here, TB), :]
        dkv_ref[b, 0:TB, :] = jnp.where(krow < size, got, 0.0).astype(BF)
        dkv_ref[b, TB : TB + EXT, :] = jnp.zeros((EXT, CH), BF)


VMEM = pl.BlockSpec(memory_space=pltpu.VMEM)
SMEM = pl.BlockSpec(memory_space=pltpu.SMEM)
PARAMS = pltpu.CompilerParams(vmem_limit_bytes=48 * 1024 * 1024)


def packed_scratch():
    return [
        pltpu.VMEM((KROWS + TB, 2 * CH), BF),
        pltpu.VMEM((CH, KROWS + TK), BF),
        pltpu.VMEM((2 * CH, QCOLS + CH), BF),
        pltpu.VMEM((2 * CH, QCOLS + CH), BF),
    ]


def forward(kv_all, x_all):
    return pl.pallas_call(
        forward_kernel,
        out_shape=jax.ShapeDtypeStruct((NY, HD + 3 * EXT, TB), BF),
        in_specs=[VMEM, VMEM],
        out_specs=VMEM,
        scratch_shapes=packed_scratch()
        + [
            pltpu.VMEM((HD, QCOLS + CH), F32),
            pltpu.VMEM((8, QCOLS + CH), F32),
            pltpu.VMEM((EXT, TB), F32),
        ],
        compiler_params=PARAMS,
        cost_estimate=pl.CostEstimate(flops=4 * 10**9, bytes_accessed=2 * 10**6, transcendentals=0),
        name="forward",
    )(kv_all, x_all)


def combine(own, got, grad_all):
    return pl.pallas_call(
        combine_kernel,
        out_shape=jax.ShapeDtypeStruct((NY * NZ, 16, CH), BF),
        in_specs=[SMEM, VMEM, VMEM],
        out_specs=VMEM,
        scratch_shapes=[pltpu.VMEM((NY, NY, TB), F32)],
        compiler_params=PARAMS,
        cost_estimate=pl.CostEstimate(flops=5 * 10**7, bytes_accessed=2 * 10**6, transcendentals=0),
        name="combine",
    )(own, got, grad_all)


def backward(kv_all, x_all, got):
    return pl.pallas_call(
        backward_kernel,
        out_shape=(
            jax.ShapeDtypeStruct((NY, NCH * HD, CH), BF),
            jax.ShapeDtypeStruct((NZ, TB + EXT, CH), BF),
        ),
        in_specs=[VMEM, VMEM, VMEM],
        out_specs=(VMEM, VMEM),
        scratch_shapes=packed_scratch()
        + [
            pltpu.VMEM((QCOLS + CH, CH), BF),
            pltpu.VMEM((QCOLS + CH, CH), BF),
            pltpu.VMEM((3, NY, TB), F32),
            pltpu.VMEM((3, NY, TB), F32),
            pltpu.VMEM((HD, QCOLS + CH), F32),
            pltpu.VMEM((KROWS + TB, CH), F32),
        ],
        compiler_params=PARAMS,
        cost_estimate=pl.CostEstimate(flops=8 * 10**9, bytes_accessed=2 * 10**6, transcendentals=0),
        name="backward",
    )(kv_all, x_all, got)


def exchange(slots, axis, groups=None):
    return lax.all_to_all(slots, axis, 0, 0, tiled=True, axis_index_groups=groups)


def spread(block, count):
    return jnp.broadcast_to(block[None], (count,) + block.shape)


def on_device(queries, keys, values, out_grad, w_out, counts, keep):
    count = counts[0]
    valid = jnp.arange(TB, dtype=jnp.int32) < count
    live = jnp.where(valid, keep, 0).astype(BF)
    grad = out_grad * live[None, :]
    step = lax.broadcasted_iota(jnp.int32, (EXT, TB), 0)
    meta = jnp.where(step == 0, count // 16, jnp.where(step == 1, count % 16, 0)).astype(BF)
    kv = jnp.concatenate([jnp.concatenate([keys, values], 0).T, meta[:, 0:CH]], 0)
    kv_all = lax.all_gather(kv, "tok", axis=0, axis_index_groups=Z_GROUPS)
    grad_all = exchange(spread(grad, 16), "head").reshape(16 * HD, TB)
    d_attn = jnp.dot(w_out, grad_all, preferred_element_type=F32).astype(BF)
    x = jnp.concatenate([queries * jnp.asarray(0.125, BF), d_attn, meta], 0)
    x_all = exchange(spread(x, NY), "tok", Y_GROUPS)
    got = exchange(forward(kv_all, x_all), "tok", Y_GROUPS)
    own = (lax.axis_index("tok") // NZ).astype(jnp.int32).reshape(1)
    parts = exchange(combine(own, got, grad_all), "tok")
    dq_parts, dkv_parts = backward(kv_all, x_all, got)
    piece = jnp.sum(parts.astype(F32), axis=0).astype(BF)
    dkv_parts = dkv_parts.at[:, TB:, :].set(piece[None])
    dkv_got = exchange(dkv_parts, "tok", Z_GROUPS)
    row_pieces = dkv_got[:, TB:, :].reshape(NZ * 16, CH)
    last = jnp.concatenate([dq_parts, spread(row_pieces, NY)], 1)
    last = exchange(last, "tok", Y_GROUPS)
    dkv = jnp.sum(dkv_got[:, 0:TB, :].astype(F32), axis=0).astype(BF).T
    dq = jnp.sum(last[:, 0 : NCH * HD].astype(F32), axis=0).astype(BF)
    dq = dq.reshape(NCH, HD, CH).transpose(1, 0, 2).reshape(HD, TB)
    d_wout = last[:, NCH * HD :].reshape(NY, NZ, 16, CH).transpose(0, 2, 1, 3).reshape(HD, 16 * HD)
    return dq, dkv[0:HD], dkv[HD:], d_wout.astype(F32)


def solution(mesh):
    return jax.shard_map(
        on_device,
        mesh=mesh,
        in_specs=(
            P("head", "tok"),
            P("head", "tok"),
            P("head", "tok"),
            P("head", "tok"),
            P("head", None),
            P("tok"),
            P("tok"),
        ),
        out_specs=(P("head", "tok"), P("head", "tok"), P("head", "tok"), P("head", None)),
        check_vma=False,
    )
```

time: 762 us -> 155 us (0.20)
  waiting for transfers between devices: 296 us -> 33.1 us
  blocking collectives: 264 us -> 51.6 us
  matrix products: 159 us -> 0.24 us
  starting transfers between devices: 0.19 us -> 40.4 us
  other arithmetic: 19.7 us -> 1.97 us
  Pallas kernels: 0 us -> 17 us
  between operations: 14.6 us -> 1.53 us
    psum x1 -> x0, waiting for transfers between devices: 234 us -> none  [on_device(): weight_grad = lax.psum(w_acc, 'tok')]
    all_gather x4 -> x1, blocking collectives: 264 us -> 31.9 us  [on_device(): kv_all = lax.all_gather(kv, 'tok', axis=0, axis_index_groups=Z_GROUPS)]
    dot_general x114 -> x1, matrix products: 159 us -> 0.24 us  [on_device(): d_attn = jnp.dot(w_out, grad_all, preferred_element_type=F32).astype(BF)]
    all_gather x4 -> x0, waiting for transfers between devices: 60 us -> none  [the longest x1 59.9 us: on_device(): lax.all_gather(values, 'tok', axis=1, tiled=True)]
    all_to_all x0 -> x5, starting transfers between devices: none -> 40.4 us  [exchange(): lax.all_to_all(slots, axis, 0, 0, tiled=True, axis_index_groups=groups)]
    all_to_all x0 -> x5, waiting for transfers between devices: none -> 33.1 us  [exchange(): lax.all_to_all(slots, axis, 0, 0, tiled=True, axis_index_groups=groups)]
    all_to_all x0 -> x1, blocking collectives: none -> 19.7 us  [exchange(): lax.all_to_all(slots, axis, 0, 0, tiled=True, axis_index_groups=groups)]
    pallas_call x0 -> x3, Pallas kernels: none -> 17 us  [the longest x1 7.95 us: backward(): pl.pallas_call(backward_kernel, out_shape=(jax.ShapeDtypeStruct((NY, NCH...]
  transfers between devices with their start and end apart: 5 -> 5, of which waited for: 2 -> 4; matrix products, arithmetic and copies ran while one was open for 24% -> 1% of each run, Pallas kernels for 0% -> 5%
where the time goes in v1:
time: 155 us; the launch traced here: 153 us
  blocking collectives  51.6 us (33%)
  starting transfers between devices  40.4 us (26%)
  waiting for transfers between devices  33.1 us (21%)
  Pallas kernels  17 us (11%)
  local copies, waits for them, and re-layouts  7.03 us (5%)
  other arithmetic  1.97 us (1%)
    all_to_all x5, starting transfers between devices, exchange(): lax.all_to_all(slots, axis, 0, 0, tiled=True, axis_index_groups=groups)  40.4 us
    all_to_all x5, waiting for transfers between devices, exchange(): lax.all_to_all(slots, axis, 0, 0, tiled=True, axis_index_groups=groups)  33.1 us
    all_gather x1, blocking collectives, on_device(): kv_all = lax.all_gather(kv, 'tok', axis=0, axis_index_groups=Z_GROUPS)  31.9 us
    all_to_all x1, blocking collectives, exchange(): lax.all_to_all(slots, axis, 0, 0, tiled=True, axis_index_groups=groups)  19.7 us
    pallas_call x1, Pallas kernels, backward(): pl.pallas_call(backward_kernel, out_shape=(jax.ShapeDtypeStruct((NY, NCH...  7.95 us
    pallas_call x1, Pallas kernels, forward(): pl.pallas_call(forward_kernel, out_shape=jax.ShapeDtypeStruct((NY, HD + 3...  7.86 us
    unnamed x17, local copies, waits for them, and re-layouts  3.79 us
  transfers between devices with their start and end apart: 5, of which 4 were waited for; matrix products, arithmetic and copies ran while one was open for 1% of the time, Pallas kernels for 5%

profile of v1, /device:TPU:6, one launch (start us, length us, event | category | flops | bytes accessed | tf_op | source)
XLA Modules:
  0.0 152.9 jit_solution(16995978342753400295)
XLA Ops:
  1.4 0.8 broadcast_multiply_fusion
  2.2 1.0 broadcast_in_dim.41
  3.2 9.3 %all-to-all-start = ((bf16[16,64,384]{2,1,0:T(8,128)(2,1)}), bf16[16,64,384]{2,1,0:T(8,128)(2,1)S(1)}, u32[]{:S(2)}, u32[]{:S(2)}) async-start(bf16[16,64,384]{2,1,0:T(8,128)(2,1)} %broadcast_in_dim.41), calls=%async_computation | async-start | bytes 1572864 | tf_op jit(solution)/shard_map/all_to_all | solution.py:337
  12.6 0.7 copy-done.2
  13.3 10.6 %all-to-all-done = bf16[16,64,384]{2,1,0:T(8,128)(2,1)S(1)} async-done(((bf16[16,64,384]{2,1,0:T(8,128)(2,1)}), bf16[16,64,384]{2,1,0:T(8,128)(2,1)S(1)}, u32[]{:S(2)}, u32[]{:S(2)}) %all-to-all-start) | async-done | bytes 786464 | tf_op jit(solution)/shard_map/all_to_all | solution.py:337
  23.9 0.2 fusion
  24.2 0.8 broadcast_in_dim.42
  25.0 3.6 %all-to-all-start.1 = ((bf16[4,144,384]{2,1,0:T(8,128)(2,1)}), bf16[4,144,384]{2,1,0:T(8,128)(2,1)S(1)}, u32[]{:S(2)}, u32[]{:S(2)}) async-start(bf16[4,144,384]{2,1,0:T(8,128)(2,1)} %broadcast_in_dim.42), calls=%async_computation.1 | async-start | bytes 884736 | tf_op jit(solution)/shard_map/all_to_all | solution.py:337
  28.6 0.1 copy.18
  28.8 0.7 copy-done.4
  29.4 0.1 copy.19
  29.6 0.1 maximum_bitcast_fusion
  29.7 0.6 slice-done
  30.3 31.9 %all-gather = bf16[3200,128]{1,0:T(8,128)(2,1)S(1)} all-gather(bf16[400,128]{1,0:T(8,128)(2,1)S(1)} %pad_maximum_fusion.2), channel_id=2, replica_groups={{0,16,32,48,64,80,96,112},{128,144,160,176,192,208,224,240},{256,272,28..., dimensions={0}, use_global_device_ids=true | all-gather | bytes 921600 | tf_op jit(solution)/shard_map/all_gather | solution.py:352
  62.2 7.9 %forward.1 = bf16[4,112,384]{2,1,0:T(8,128)(2,1)} custom-call(bf16[8,400,128]{2,1,0:T(8,128)(2,1)S(1)} %bitcast.35, bf16[4,144,384]{2,1,0:T(8,128)(2,1)S(1)} %all-to-all-done.1.x_ref), custom_call_target="tpu_custom_call" | custom-call | flops 4000000000 | bytes 2000000 | tf_op jit(solution)/shard_map/forward/pallas_call | solution.py:282
  70.0 8.8 %all-to-all-start.2 = ((bf16[4,112,384]{2,1,0:T(8,128)(2,1)}), bf16[4,112,384]{2,1,0:T(8,128)(2,1)S(1)}, u32[]{:S(2)}, u32[]{:S(2)}) async-start(bf16[4,112,384]{2,1,0:T(8,128)(2,1)} %forward.1), calls=%async_computation.2 | async-start | bytes 688128 | tf_op jit(solution)/shard_map/all_to_all | solution.py:337
  78.8 9.6 %all-to-all-done.2.r_ref = bf16[4,112,384]{2,1,0:T(8,128)(2,1)S(1)} async-done(((bf16[4,112,384]{2,1,0:T(8,128)(2,1)}), bf16[4,112,384]{2,1,0:T(8,128)(2,1)S(1)}, u32[]{:S(2)}, u32[]{:S(2)}) %all-to-all-start.2) | async-done | bytes 344096 | tf_op jit(solution)/shard_map/all_to_all | solution.py:337
  88.4 1.1 combine.1
  89.5 9.7 %all-to-all-start.3 = ((bf16[32,16,128]{2,1,0:T(8,128)(2,1)}), bf16[32,16,128]{2,1,0:T(8,128)(2,1)S(1)}, u32[]{:S(2)}, u32[]{:S(2)}) async-start(bf16[32,16,128]{2,1,0:T(8,128)(2,1)} %combine.1), calls=%async_computation.3 | async-start | bytes 262144 | tf_op jit(solution)/shard_map/all_to_all | solution.py:337
  99.2 8.0 %backward.1 = (bf16[4,192,128]{2,1,0:T(8,128)(2,1)S(1)}, bf16[8,400,128]{2,1,0:T(8,128)(2,1)S(1)}) custom-call(bf16[8,400,128]{2,1,0:T(8,128)(2,1)S(1)} %bitcast.36, bf16[4,144,384]{2,1,0:T(8,128)(2,1)S(1)} %all-to-all-done.1.x_ref, bf16[4,112,384]{2,1,0:T(8,128)(2,1)S(1)} %all-to-all-done.2.r_ref), custom_call_target="tpu_custom_call" | custom-call | flops 8000000000 | bytes 2000000 | tf_op jit(solution)/shard_map/backward/pallas_call | solution.py:313
  107.2 4.7 %all-to-all-done.3 = bf16[32,16,128]{2,1,0:T(8,128)(2,1)S(1)} async-done(((bf16[32,16,128]{2,1,0:T(8,128)(2,1)}), bf16[32,16,128]{2,1,0:T(8,128)(2,1)S(1)}, u32[]{:S(2)}, u32[]{:S(2)}) %all-to-all-start.3) | async-done | bytes 131104 | tf_op jit(solution)/shard_map/all_to_all | solution.py:337
  112.0 19.7 %all_to_all.30 = bf16[8,400,128]{2,1,0:T(8,128)(2,1)S(1)} all-to-all(bf16[8,400,128]{2,1,0:T(8,128)(2,1)S(1)} %broadcast_dynamic-update-slice_fusion), channel_id=1, replica_groups={{0,16,32,48,64,80,96,112},{128,144,160,176,192,208,224,240},{256,272,28..., dimensions={0} | all-to-all | bytes 1638400 | tf_op jit(solution)/shard_map/all_to_all | solution.py:337
  131.7 0.7 pad_maximum_fusion
  132.5 9.0 %all-to-all-start.5 = ((bf16[4,320,128]{2,1,0:T(8,128)(2,1)}), bf16[4,320,128]{2,1,0:T(8,128)(2,1)S(1)}, u32[]{:S(2)}, u32[]{:S(2)}) async-start(bf16[4,320,128]{2,1,0:T(8,128)(2,1)} %pad_maximum_fusion), calls=%async_computation.5 | async-start | bytes 655360 | tf_op jit(solution)/shard_map/all_to_all | solution.py:337
  141.5 0.1 slice_reduce_fusion
  141.6 0.1 fusion.1
  141.7 0.7 copy.22
  142.4 0.7 copy.23
  143.2 8.2 %all-to-all-done.5 = bf16[4,320,128]{2,1,0:T(8,128)(2,1)S(1)} async-done(((bf16[4,320,128]{2,1,0:T(8,128)(2,1)}), bf16[4,320,128]{2,1,0:T(8,128)(2,1)S(1)}, u32[]{:S(2)}, u32[]{:S(2)}) %all-to-all-start.5) | async-done | bytes 327712 | tf_op jit(solution)/shard_map/all_to_all | solution.py:337
  151.4 0.1 copy.21
  151.5 0.8 copy.28
  152.2 0.6 copy.29
  (26 shorter events, 0.3 us)
Async XLA Ops:
  0.6 23.3 %copy-start = (bf16[64,1024]{1,0:T(8,128)(2,1)S(1)}, bf16[64,1024]{1,0:T(8,128)(2,1)}, u32[]{:S(2)}) copy-start(bf16[64,1024]{1,0:T(8,128)(2,1)} %param.13) | copy-start | bytes 393220
  0.6 0.7 copy-start.5
  3.2 20.7 %all-to-all-start = ((bf16[16,64,384]{2,1,0:T(8,128)(2,1)}), bf16[16,64,384]{2,1,0:T(8,128)(2,1)S(1)}, u32[]{:S(2)}, u32[]{:S(2)}) async-start(bf16[16,64,384]{2,1,0:T(8,128)(2,1)} %broadcast_in_dim.41), calls=%async_computation | async-start | bytes 1572864 | tf_op jit(solution)/shard_map/all_to_all | solution.py:337
  12.5 0.8 copy-start.2
  13.3 15.3 %copy-start.1 = (bf16[16,384]{1,0:T(8,128)(2,1)}, bf16[16,384]{1,0:T(8,128)(2,1)S(1)}, u32[]{:S(2)}) copy-start(bf16[16,384]{1,0:T(8,128)(2,1)S(1)} %select_convert_fusion) | copy-start | bytes 36868
  25.0 3.6 %copy-start.3 = (bf16[64,384]{1,0:T(8,128)(2,1)S(1)}, bf16[64,384]{1,0:T(8,128)(2,1)}, u32[]{:S(2)}) copy-start(bf16[64,384]{1,0:T(8,128)(2,1)} %param.10) | copy-start | bytes 147460
  25.0 37.2 %all-to-all-start.1 = ((bf16[4,144,384]{2,1,0:T(8,128)(2,1)}), bf16[4,144,384]{2,1,0:T(8,128)(2,1)S(1)}, u32[]{:S(2)}, u32[]{:S(2)}) async-start(bf16[4,144,384]{2,1,0:T(8,128)(2,1)} %broadcast_in_dim.42), calls=%async_computation.1 | async-start | bytes 884736 | tf_op jit(solution)/shard_map/all_to_all | solution.py:337
  28.6 0.8 copy-start.4
  29.6 0.7 slice-start
  70.0 18.3 %all-to-all-start.2 = ((bf16[4,112,384]{2,1,0:T(8,128)(2,1)}), bf16[4,112,384]{2,1,0:T(8,128)(2,1)S(1)}, u32[]{:S(2)}, u32[]{:S(2)}) async-start(bf16[4,112,384]{2,1,0:T(8,128)(2,1)} %forward.1), calls=%async_computation.2 | async-start | bytes 688128 | tf_op jit(solution)/shard_map/all_to_all | solution.py:337
  89.5 22.4 %all-to-all-start.3 = ((bf16[32,16,128]{2,1,0:T(8,128)(2,1)}), bf16[32,16,128]{2,1,0:T(8,128)(2,1)S(1)}, u32[]{:S(2)}, u32[]{:S(2)}) async-start(bf16[32,16,128]{2,1,0:T(8,128)(2,1)} %combine.1), calls=%async_computation.3 | async-start | bytes 262144 | tf_op jit(solution)/shard_map/all_to_all | solution.py:337
  132.5 18.8 %all-to-all-start.5 = ((bf16[4,320,128]{2,1,0:T(8,128)(2,1)}), bf16[4,320,128]{2,1,0:T(8,128)(2,1)S(1)}, u32[]{:S(2)}, u32[]{:S(2)}) async-start(bf16[4,320,128]{2,1,0:T(8,128)(2,1)} %pad_maximum_fusion), calls=%async_computation.5 | async-start | bytes 655360 | tf_op jit(solution)/shard_map/all_to_all | solution.py:337

commit v2 on v1

v2 whole, which is shorter than its diff:
```python
import jax
import jax.numpy as jnp
from jax import lax
from jax.experimental import pallas as pl
from jax.experimental.pallas import tpu as pltpu
from jax.sharding import PartitionSpec as P

HD = 64
D = 1024
TB = 384
NY = 4
NZ = 8
CH = 128
NCH = TB // CH
TK = 256
TQ = 256
KROWS = NZ * TB
QCOLS = NY * TB
KPAD = KROWS + TB
QPAD = QCOLS + CH
WIDE = TB + CH
EXT = 16
BIAS = -30000.0
BF = jnp.bfloat16
F32 = jnp.float32
Z_GROUPS = [[y * NZ + z for z in range(NZ)] for y in range(NY)]
Y_GROUPS = [[y * NZ + z for y in range(NY)] for z in range(NZ)]
KEY_AT, KEY_SIZE, QUERY_AT, QUERY_SIZE, KEY_TILES, QUERY_TILES = 0, 8, 16, 20, 24, 25


def dot(a, b):
    return jnp.dot(a, b, preferred_element_type=F32)


def dot_nt(a, b):
    return lax.dot_general(a, b, (((1,), (1,)), ((), ())), preferred_element_type=F32)


def iota(shape, dim):
    return lax.broadcasted_iota(jnp.int32, shape, dim)


def eye(n):
    return jnp.where(iota((n, n), 0) == iota((n, n), 1), 1.0, 0.0).astype(BF)


def pieces(x):
    hi = x.astype(BF)
    rest = x - hi.astype(F32)
    mid = rest.astype(BF)
    low = (rest - mid.astype(F32)).astype(BF)
    return hi, mid, low


def two_rows(shape, first, second):
    row = iota(shape, 0)
    return jnp.where(row == 0, first, jnp.where(row == 1, second, 0.0)).astype(BF)


def count_of(meta):
    meta = meta.astype(F32)
    return jnp.max(meta[0:1, 0:CH] * 16.0 + meta[1:2, 0:CH]).astype(jnp.int32)


def place_matrix(spot):
    return jnp.where(iota((TB, TB), 0).astype(F32) == spot, 1.0, 0.0).astype(BF)


def prepare_kernel(count_ref, keys_ref, values_ref, out_grad_ref, keep_ref, kv_ref, grad_ref, spot_ref):
    count = count_ref[0]
    live = jnp.where(iota((8, TB), 1) < count, keep_ref[...].astype(F32), 0.0)
    grad_ref[...] = out_grad_ref[...] * live[0:1].astype(BF)
    upto = jnp.where(iota((TB, TB), 0) <= iota((TB, TB), 1), 1.0, 0.0).astype(BF)
    order = dot(live.astype(BF), upto)
    spot_ref[...] = jnp.where(live > 0.0, order - 1.0, -1.0)
    both = jnp.concatenate([keys_ref[...], values_ref[...]], 0)
    turned = dot_nt(eye(TB), both).astype(BF)
    high = (count // 16).astype(F32)
    low = (count % 16).astype(F32)
    meta = two_rows((EXT, CH), high, low)
    for z in range(NZ):
        kv_ref[z, 0:TB, :] = turned
        kv_ref[z, TB : TB + EXT, :] = meta


def project_kernel(w_ref, grad_ref, queries_ref, spot_ref, _, x_ref):
    d_attn = dot(w_ref[...], grad_ref[...]).astype(BF)
    spot = spot_ref[0:1, :]
    place = place_matrix(spot)
    queries = queries_ref[...] * jnp.asarray(0.125, BF)
    x = dot_nt(jnp.concatenate([queries, d_attn], 0), place).astype(BF)
    n = jnp.max(spot, axis=1, keepdims=True) + 1.0
    high = jnp.floor(n / 16.0)
    meta = two_rows((EXT, TB), high, n - 16.0 * high)
    for y in range(NY):
        x_ref[y, 0 : 2 * HD, :] = x
        x_ref[y, 2 * HD : 2 * HD + EXT, :] = meta


def pack_keys(kv_ref, kvp_ref, sc_ref):
    lane = iota((TB, CH), 1)
    row = iota((TB, CH), 0)
    ones = jnp.where((lane >= 1) & (lane <= 3), 1.0, 0.0)
    offset = jnp.int32(0)
    for b in range(NZ):
        count = count_of(kv_ref[b, TB : TB + EXT, :])
        here = pl.multiple_of(offset, 16)
        kvp_ref[pl.ds(here, TB), 0:CH] = kv_ref[b, 0:TB, :]
        aux = jnp.where((lane == 0) & (row >= count), BIAS, ones)
        kvp_ref[pl.ds(here, TB), CH : 2 * CH] = aux.astype(BF)
        size = ((count + 15) // 16) * 16
        sc_ref[KEY_AT + b] = offset
        sc_ref[KEY_SIZE + b] = size
        offset = offset + size
    here = pl.multiple_of(offset, 16)
    kvp_ref[pl.ds(here, TK), 0:CH] = jnp.zeros((TK, CH), BF)
    kvp_ref[pl.ds(here, TK), CH : 2 * CH] = jnp.where(lane == 0, BIAS, ones)[0:TK].astype(BF)
    n_tiles = (offset + TK - 1) // TK
    sc_ref[KEY_TILES] = n_tiles
    return n_tiles


def transpose_keys(kvp_ref, kvt_ref, n_key_tiles):
    unit = eye(CH)
    kvt_ref[CH : CH + EXT, :] = jnp.where(iota((EXT, KPAD), 0) == 0, 1.0, 0.0).astype(BF)

    def one(kt, _):
        at = pl.multiple_of(kt * TK, TK)
        kvt_ref[0:CH, pl.ds(at, TK)] = dot_nt(unit, kvp_ref[pl.ds(at, TK), 0:CH]).astype(BF)
        return 0

    lax.fori_loop(0, n_key_tiles, one, 0)


def lane_window(offset):
    start = (offset // CH) * CH
    return pl.multiple_of(start, CH), offset - start


def pack_queries(x_ref, xp_ref, sc_ref):
    xp_ref[...] = jnp.zeros(xp_ref.shape, F32)
    offset = jnp.int32(0)
    for b in range(NY):
        count = count_of(x_ref[b, 2 * HD : 2 * HD + EXT, :])
        start, shift = lane_window(offset)
        block = x_ref[b, 0 : 2 * HD, :].astype(F32)
        block = jnp.concatenate([block, jnp.zeros((2 * HD, CH), F32)], 1)
        xp_ref[:, pl.ds(start, WIDE)] += pltpu.roll(block, shift, 1)
        sc_ref[QUERY_AT + b] = offset
        sc_ref[QUERY_SIZE + b] = count
        offset = offset + count
    n_tiles = (offset + TQ - 1) // TQ
    sc_ref[QUERY_TILES] = n_tiles
    return n_tiles


def unpack_lanes(window, shift, count):
    back = pltpu.roll(window, (WIDE - shift) % WIDE, 1)[:, 0:TB]
    return jnp.where(iota(back.shape, 1) < count, back, 0.0)


def over_keys(n_key_tiles, step, state):
    big = n_key_tiles // 4
    state = lax.fori_loop(0, big, lambda i, s: step(i * 4 * TK, 4 * TK, s), state)
    half = (n_key_tiles // 2) % 2
    state = lax.fori_loop(0, half, lambda i, s: step(big * 4 * TK, 2 * TK, s), state)
    last = n_key_tiles % 2
    return lax.fori_loop(0, last, lambda i, s: step((n_key_tiles - 1) * TK, TK, s), state)


def forward_kernel(kv_ref, x_ref, out_ref, sc_ref, kvp_ref, kvt_ref, xp_ref, ws_ref, acc_ref, st_ref):
    n_key_tiles = pack_keys(kv_ref, kvp_ref, sc_ref)
    transpose_keys(kvp_ref, kvt_ref, n_key_tiles)
    n_query_tiles = pack_queries(x_ref, xp_ref, sc_ref)
    ws_ref[...] = jnp.zeros(ws_ref.shape, BF)
    ws_ref[0:HD, :] = xp_ref[0:HD, :].astype(BF)
    ws_ref[CH : CH + EXT, :] = jnp.where(iota((EXT, QPAD), 0) == 0, 1.0, 0.0).astype(BF)
    st_ref[...] = jnp.where(iota((8, QPAD), 0) == 1, 1.0, 0.0)
    acc_ref[...] = jnp.zeros(acc_ref.shape, F32)

    def query_tile(qt, _):
        q0 = pl.multiple_of(qt * TQ, TQ)
        ws = ws_ref[:, pl.ds(q0, TQ)]

        def key_tile(k0, size, carry):
            top, acc = carry
            k0 = pl.multiple_of(k0, TK)
            s = dot(kvp_ref[pl.ds(k0, size), :], ws)
            new = jnp.maximum(top, jnp.max(s, axis=0, keepdims=True))
            e = jnp.exp(s - new).astype(BF)
            acc = acc * jnp.exp(top - new) + dot(kvt_ref[HD : CH + EXT, pl.ds(k0, size)], e)
            return new, acc

        start = (jnp.full((1, TQ), -1e30, F32), jnp.zeros((HD + EXT, TQ), F32))
        top, acc = over_keys(n_key_tiles, key_tile, start)
        total = acc[HD : HD + 1]
        dsum = jnp.sum(acc[0:HD] * xp_ref[HD : 2 * HD, pl.ds(q0, TQ)], axis=0, keepdims=True)
        acc_ref[:, pl.ds(q0, TQ)] = acc[0:HD] / total
        st_ref[0:1, pl.ds(q0, TQ)] = top
        st_ref[1:2, pl.ds(q0, TQ)] = total
        st_ref[2:3, pl.ds(q0, TQ)] = dsum
        return 0

    lax.fori_loop(0, n_query_tiles, query_tile, 0)

    rows = [st_ref[i : i + 1, q * TB : (q + 1) * TB] for i in range(3) for q in range(NY)]
    split = pieces(jnp.concatenate(rows + [jnp.zeros((4, TB), F32)], 0))
    for b in range(NY):
        start, shift = lane_window(sc_ref[QUERY_AT + b])
        part = unpack_lanes(acc_ref[:, pl.ds(start, WIDE)], shift, sc_ref[QUERY_SIZE + b])
        out_ref[b, 0:HD, :] = part.astype(BF)
        for i in range(3):
            out_ref[b, HD + i * EXT : HD + (i + 1) * EXT, :] = split[i]


def merged_stats(r_ref):
    stats = []
    for s in range(NY):
        st = r_ref[s, HD : HD + EXT, :].astype(F32)
        st = st + r_ref[s, HD + EXT : HD + 2 * EXT, :].astype(F32)
        stats.append(st + r_ref[s, HD + 2 * EXT : HD + 3 * EXT, :].astype(F32))
    top = stats[0][0:NY]
    for s in range(1, NY):
        top = jnp.maximum(top, stats[s][0:NY])
    shares = []
    total = jnp.zeros((NY, TB), F32)
    dsum = jnp.zeros((NY, TB), F32)
    for s in range(NY):
        fade = jnp.exp(stats[s][0:NY] - top)
        shares.append(stats[s][NY : 2 * NY] * fade)
        total = total + shares[s]
        dsum = dsum + stats[s][2 * NY : 3 * NY] * fade
    return top + jnp.log(total), dsum / total, [share / total for share in shares]


def combine_kernel(y_ref, sc_ref, r_ref, grad_ref, spot_ref, out_ref, share_ref):
    _, _, shares = merged_stats(r_ref)
    share_ref[...] = jnp.zeros(share_ref.shape, F32)
    for s in range(NY):
        for q in range(NY):
            share_ref[s : s + 1, q * TB : (q + 1) * TB] = shares[s][q : q + 1]
    own = y_ref[0]
    start, shift = lane_window(sc_ref[QUERY_AT + own])
    share = unpack_lanes(share_ref[:, pl.ds(start, WIDE)], shift, sc_ref[QUERY_SIZE + own])
    attn = jnp.zeros((HD, TB), F32)
    for s in range(NY):
        attn = attn + r_ref[s, 0:HD, :].astype(F32) * share[s : s + 1]
    attn = dot(attn.astype(BF), place_matrix(spot_ref[0:1, :])).astype(BF)
    for z in range(NZ):
        part = dot_nt(attn, grad_ref[z * CH : (z + 1) * CH, :])
        for y in range(NY):
            out_ref[y * NZ + z] = part[y * 16 : (y + 1) * 16, :].astype(BF)


def backward_kernel(
    kv_ref, x_ref, r_ref, dq_ref, dkv_ref, sc_ref, kvp_ref, kvt_ref, xp_ref, ws_ref, wd_ref, xq_ref, xd_ref, dqa_ref, dkva_ref
):
    n_key_tiles = pack_keys(kv_ref, kvp_ref, sc_ref)
    transpose_keys(kvp_ref, kvt_ref, n_key_tiles)
    n_query_tiles = pack_queries(x_ref, xp_ref, sc_ref)
    ws_ref[...] = jnp.zeros(ws_ref.shape, BF)
    wd_ref[...] = jnp.zeros(wd_ref.shape, BF)
    ws_ref[0:HD, :] = xp_ref[0:HD, :].astype(BF)
    wd_ref[HD : 2 * HD, :] = xp_ref[HD : 2 * HD, :].astype(BF)
    lse, delta, _ = merged_stats(r_ref)
    row = iota((EXT, TB), 0)
    lse_pieces = [piece.astype(F32) for piece in pieces(-lse)]
    delta_pieces = [piece.astype(F32) for piece in pieces(-delta)]
    for q in range(NY):
        tile_s = jnp.where(row == 0, 1.0, 0.0)
        tile_d = jnp.zeros((EXT, TB), F32)
        for i in range(3):
            tile_s = jnp.where(row == i + 1, lse_pieces[i][q : q + 1], tile_s)
            tile_d = jnp.where(row == i + 1, delta_pieces[i][q : q + 1], tile_d)
        ws_ref[CH : CH + EXT, q * TB : (q + 1) * TB] = tile_s.astype(BF)
        wd_ref[CH : CH + EXT, q * TB : (q + 1) * TB] = tile_d.astype(BF)

    unit = eye(TQ)

    def turn(qt, _):
        q0 = pl.multiple_of(qt * TQ, TQ)
        xq_ref[pl.ds(q0, TQ), :] = dot_nt(unit, ws_ref[0:CH, pl.ds(q0, TQ)]).astype(BF)
        xd_ref[pl.ds(q0, TQ), :] = dot_nt(unit, wd_ref[0:CH, pl.ds(q0, TQ)]).astype(BF)
        return 0

    lax.fori_loop(0, n_query_tiles, turn, 0)
    dqa_ref[...] = jnp.zeros(dqa_ref.shape, F32)

    def key_tile(k0, size, _):
        k0 = pl.multiple_of(k0, TK)
        kv = kvp_ref[pl.ds(k0, size), :]
        dkva_ref[pl.ds(k0, size), :] = jnp.zeros((size, CH), F32)

        def query_tile(qt, _):
            q0 = pl.multiple_of(qt * TQ, TQ)
            prob = jnp.exp(dot(kv, ws_ref[:, pl.ds(q0, TQ)]))
            dscore = (prob * dot(kv, wd_ref[:, pl.ds(q0, TQ)])).astype(BF)
            prob = prob.astype(BF)
            dqa_ref[:, pl.ds(q0, TQ)] += dot(kvt_ref[0:HD, pl.ds(k0, size)], dscore)
            acc = dot(dscore, xq_ref[pl.ds(q0, TQ), :]) + dot(prob, xd_ref[pl.ds(q0, TQ), :])
            dkva_ref[pl.ds(k0, size), :] += acc
            return 0

        lax.fori_loop(0, n_query_tiles, query_tile, 0)
        return 0

    over_keys(n_key_tiles, key_tile, 0)

    for b in range(NY):
        start, shift = lane_window(sc_ref[QUERY_AT + b])
        part = unpack_lanes(dqa_ref[:, pl.ds(start, WIDE)], shift, sc_ref[QUERY_SIZE + b])
        part = (0.125 * part).astype(BF)
        for c in range(NCH):
            dq_ref[b, c * HD : (c + 1) * HD, :] = part[:, c * CH : (c + 1) * CH]
    krow = iota((TB, CH), 0)
    for b in range(NZ):
        got = dkva_ref[pl.ds(pl.multiple_of(sc_ref[KEY_AT + b], 16), TB), :]
        dkv_ref[b, 0:TB, :] = jnp.where(krow < sc_ref[KEY_SIZE + b], got, 0.0).astype(BF)
        dkv_ref[b, TB : TB + EXT, :] = jnp.zeros((EXT, CH), BF)


def keys_out_kernel(got_ref, dk_ref, dv_ref):
    total = got_ref[0, 0:TB, :].astype(F32)
    for z in range(1, NZ):
        total = total + got_ref[z, 0:TB, :].astype(F32)
    turned = dot_nt(eye(CH), total.astype(BF)).astype(BF)
    dk_ref[...] = turned[0:HD]
    dv_ref[...] = turned[HD:]


def rest_out_kernel(got_ref, spot_ref, dq_ref, dw_ref):
    place = place_matrix(spot_ref[0:1, :])
    total = got_ref[0, 0 : NCH * HD, :].astype(F32)
    for y in range(1, NY):
        total = total + got_ref[y, 0 : NCH * HD, :].astype(F32)
    total = total.astype(BF)
    dq = dot(total[0:HD], place[0:CH])
    for c in range(1, NCH):
        dq = dq + dot(total[c * HD : (c + 1) * HD], place[c * CH : (c + 1) * CH])
    dq_ref[...] = dq.astype(BF)
    base = NCH * HD
    for y in range(NY):
        for z in range(NZ):
            part = got_ref[y, base + z * 16 : base + (z + 1) * 16, :]
            dw_ref[y * 16 : (y + 1) * 16, z * CH : (z + 1) * CH] = part.astype(F32)


VMEM = pl.BlockSpec(memory_space=pltpu.VMEM)
BLOCK = pl.BlockSpec()
SMEM = pl.BlockSpec(memory_space=pltpu.SMEM)
ANY = pl.BlockSpec(memory_space=pl.ANY)
MIB = 1024 * 1024


def call(kernel, name, outs, ins, out_spaces, scratch, flops, args, limit=8):
    return pl.pallas_call(
        kernel,
        out_shape=tuple(jax.ShapeDtypeStruct(s, d) for s, d in outs),
        in_specs=ins,
        out_specs=tuple(out_spaces),
        scratch_shapes=[pltpu.VMEM(s, d) for s, d in scratch],
        compiler_params=pltpu.CompilerParams(vmem_limit_bytes=limit * MIB),
        cost_estimate=pl.CostEstimate(flops=flops, bytes_accessed=10**6, transcendentals=0),
        name=name,
    )(*args)


def prepare(count, keys, values, out_grad, keep):
    outs = [((NZ, TB + EXT, CH), BF), ((HD, TB), BF), ((8, TB), F32)]
    args = (count, keys, values, out_grad, keep)
    return call(prepare_kernel, "prepare", outs, [SMEM] + [BLOCK] * 3 + [VMEM], [VMEM] * 3, [], 10**8, args)


def project(w_out, grad_all, queries, spot, after):
    outs = [((NY, 2 * HD + EXT, TB), BF)]
    args = (w_out, grad_all, queries, spot, after)
    return call(project_kernel, "project", outs, [BLOCK, VMEM, BLOCK, VMEM, ANY], [VMEM], [], 10**8, args)[0]


PACKED = [((KPAD, 2 * CH), BF), ((CH + EXT, KPAD), BF), ((2 * HD, QPAD), F32), ((2 * CH, QPAD), BF)]


def forward(kv_all, x_all):
    outs = [((NY, HD + 3 * EXT, TB), BF), ((32,), jnp.int32)]
    scratch = PACKED + [((HD, QPAD), F32), ((8, QPAD), F32)]
    args = (kv_all, x_all)
    return call(forward_kernel, "forward", outs, [VMEM] * 2, [VMEM, SMEM], scratch, 4 * 10**9, args, 20)


def combine(own, sc, got, grad_all, spot):
    outs = [((NY * NZ, 16, CH), BF)]
    args = (own, sc, got, grad_all, spot)
    return call(combine_kernel, "combine", outs, [SMEM] * 2 + [VMEM] * 3, [VMEM], [((8, QPAD), F32)], 10**8, args)[0]


def backward(kv_all, x_all, got):
    outs = [((NY, NCH * HD, CH), BF), ((NZ, TB + EXT, CH), BF), ((32,), jnp.int32)]
    scratch = PACKED + [
        ((2 * CH, QPAD), BF),
        ((QPAD, CH), BF),
        ((QPAD, CH), BF),
        ((HD, QPAD), F32),
        ((KPAD, CH), F32),
    ]
    args = (kv_all, x_all, got)
    return call(backward_kernel, "backward", outs, [VMEM] * 3, [VMEM] * 2 + [SMEM], scratch, 8 * 10**9, args, 20)


def keys_out(got):
    outs = [((HD, TB), BF), ((HD, TB), BF)]
    return call(keys_out_kernel, "keys_out", outs, [VMEM], [VMEM] * 2, [], 10**7, (got,))


def rest_out(got, spot):
    outs = [((HD, TB), BF), ((HD, D), F32)]
    return call(rest_out_kernel, "rest_out", outs, [VMEM] * 2, [VMEM] * 2, [], 10**7, (got, spot))


def exchange(slots, axis, groups=None):
    return lax.all_to_all(slots, axis, 0, 0, tiled=True, axis_index_groups=groups)


def on_device(queries, keys, values, out_grad, w_out, counts, keep):
    kv, grad, spot = prepare(counts, keys, values, out_grad, keep.reshape(1, TB))
    kv_all = exchange(kv, "tok", Z_GROUPS)
    grad_all = lax.all_gather(grad, "head", axis=0, tiled=True)
    x_all = exchange(project(w_out, grad_all, queries, spot, kv_all), "tok", Y_GROUPS)
    slots, sc = forward(kv_all, x_all)
    got = exchange(slots, "tok", Y_GROUPS)
    own = (lax.axis_index("tok") // NZ).astype(jnp.int32).reshape(1)
    parts = exchange(combine(own, sc, got, grad_all, spot), "tok")
    dq_parts, dkv_parts, _ = backward(kv_all, x_all, got)
    piece = jnp.sum(parts.astype(F32), axis=0).astype(BF)
    dkv_parts = dkv_parts.at[:, TB:, :].set(piece[None])
    dkv_got = exchange(dkv_parts, "tok", Z_GROUPS)
    row_pieces = dkv_got[:, TB:, :].reshape(1, NZ * 16, CH)
    last = jnp.concatenate([dq_parts, jnp.broadcast_to(row_pieces, (NY, NZ * 16, CH))], 1)
    last = exchange(last, "tok", Y_GROUPS)
    dk, dv = keys_out(dkv_got)
    dq, d_wout = rest_out(last, spot)
    return dq, dk, dv, d_wout


def solution(mesh):
    return jax.shard_map(
        on_device,
        mesh=mesh,
        in_specs=(
            P("head", "tok"),
            P("head", "tok"),
            P("head", "tok"),
            P("head", "tok"),
            P("head", None),
            P("tok"),
            P("tok"),
        ),
        out_specs=(P("head", "tok"), P("head", "tok"), P("head", "tok"), P("head", None)),
        check_vma=False,
    )
```

time: 155 us -> 145 us (0.935); the launches traced: 153 us -> 145 us
  starting transfers between devices: 40.4 us -> 24.1 us
  blocking collectives: 51.6 us -> 66.9 us
  waiting for transfers between devices: 33.1 us -> 24.7 us
  Pallas kernels: 17 us -> 23.8 us
  local copies, waits for them, and re-layouts: 7.03 us -> 3.12 us
    all_to_all x1 -> x2, blocking collectives: 19.7 us -> 45.7 us  [exchange(): lax.all_to_all(slots, axis, 0, 0, tiled=True, axis_index_groups=groups)]
    all_to_all x5 -> x4, starting transfers between devices: 40.4 us -> 24.1 us  [exchange(): lax.all_to_all(slots, axis, 0, 0, tiled=True, axis_index_groups=groups)]
    all_gather x1, blocking collectives: 31.9 us -> 21.2 us  [on_device(): grad_all = lax.all_gather(grad, 'head', axis=0, tiled=True)]
    all_to_all x5 -> x4, waiting for transfers between devices: 33.1 us -> 24.7 us  [exchange(): lax.all_to_all(slots, axis, 0, 0, tiled=True, axis_index_groups=groups)]
    pallas_call x3 -> x7, Pallas kernels: 17 us -> 23.8 us  [call(): pl.pallas_call(kernel, out_shape=tuple((jax.ShapeDtypeStruct(s, d) for s,...]
    broadcast_in_dim x3 -> x1, local copies, waits for them, and re-layouts: 1.81 us -> 0.02 us  [on_device(): jnp.broadcast_to(row_pieces, (NY, NZ * 16, CH))]
    unnamed x17 -> x10, local copies, waits for them, and re-layouts: 3.79 us -> 2.4 us
  transfers between devices with their start and end apart: 5 -> 4, of which waited for: 4 -> 4; matrix products, arithmetic and copies ran while one was open for 1% -> 0% of each run, Pallas kernels for 5% -> 8%
where the time goes in v2:
time: 145 us
  blocking collectives  66.9 us (46%)
  waiting for transfers between devices  24.7 us (17%)
  starting transfers between devices  24.1 us (17%)
  Pallas kernels  23.8 us (16%)
  local copies, waits for them, and re-layouts  3.12 us (2%)
    all_to_all x2, blocking collectives, exchange(): lax.all_to_all(slots, axis, 0, 0, tiled=True, axis_index_groups=groups)  45.7 us
    all_to_all x4, waiting for transfers between devices, exchange(): lax.all_to_all(slots, axis, 0, 0, tiled=True, axis_index_groups=groups)  24.7 us
    all_to_all x4, starting transfers between devices, exchange(): lax.all_to_all(slots, axis, 0, 0, tiled=True, axis_index_groups=groups)  24.1 us
    pallas_call x7, Pallas kernels, call(): pl.pallas_call(kernel, out_shape=tuple((jax.ShapeDtypeStruct(s, d) for s,...  23.8 us
    all_gather x1, blocking collectives, on_device(): grad_all = lax.all_gather(grad, 'head', axis=0, tiled=True)  21.2 us
  transfers between devices with their start and end apart: 4, of which 4 were waited for; matrix products, arithmetic and copies ran while one was open for 0% of the time, Pallas kernels for 8%

profile of v2, /device:TPU:6, one launch (start us, length us, event | category | flops | bytes accessed | tf_op | source)
XLA Modules:
  0.0 144.7 jit_solution(965693408817551994)
XLA Ops:
  0.6 0.7 reshape.46.keep_ref
  2.0 0.0 copy-start.2
  2.0 0.8 copy-done.2
  2.8 0.0 copy-start.3
  2.8 0.8 copy-done.3
  3.6 0.0 copy-start.4
  3.6 0.8 copy-done.4
  4.4 1.2 prepare.1
  5.6 10.3 %all-to-all-start = ((bf16[8,400,128]{2,1,0:T(8,128)(2,1)}), bf16[8,400,128]{2,1,0:T(8,128)(2,1)S(1)}, u32[]{:S(2)}, u32[]{:S(2)}) async-start(bf16[8,400,128]{2,1,0:T(8,128)(2,1)} %get-tuple-element.27), calls=%async_computation | async-start | bytes 1638400 | tf_op jit(solution)/shard_map/all_to_all | solution.py:420
  15.9 0.0 copy-start
  15.9 0.0 copy-start.1
  15.9 21.2 %all_gather.3.grad_ref = bf16[1024,384]{1,0:T(8,128)(2,1)S(1)} all-gather(bf16[64,384]{1,0:T(8,128)(2,1)S(1)} %get-tuple-element.28), channel_id=1, replica_groups=mesh['tok'=32,'head'=16] {'head'}, dimensions={0}, use_global_device_ids=true | all-gather | bytes 835584 | tf_op jit(solution)/shard_map/all_gather | solution.py:426
  37.1 2.6 %all-to-all-done._.kv_ref = bf16[8,400,128]{2,1,0:T(8,128)(2,1)S(1)} async-done(((bf16[8,400,128]{2,1,0:T(8,128)(2,1)}), bf16[8,400,128]{2,1,0:T(8,128)(2,1)S(1)}, u32[]{:S(2)}, u32[]{:S(2)}) %all-to-all-start) | async-done | bytes 819232 | tf_op jit(solution)/shard_map/all_to_all | solution.py:420
  39.7 0.0 copy-done
  39.7 0.0 copy-done.1
  39.7 0.4 project.1
  40.1 21.9 %all_to_all.30.x_ref = bf16[4,144,384]{2,1,0:T(8,128)(2,1)S(1)} all-to-all(bf16[4,144,384]{2,1,0:T(8,128)(2,1)S(1)} %project.1), channel_id=1, replica_groups={{0,128,256,384},{16,144,272,400},{32,160,288,416},{48,176,304,432},{64,..., dimensions={0} | all-to-all | bytes 884736 | tf_op jit(solution)/shard_map/all_to_all | solution.py:420
  62.0 8.2 %forward.1 = (bf16[4,112,384]{2,1,0:T(8,128)(2,1)}, s32[32]{0:T(128)S(1)}) custom-call(bf16[8,400,128]{2,1,0:T(8,128)(2,1)S(1)} %all-to-all-done._.kv_ref, bf16[4,144,384]{2,1,0:T(8,128)(2,1)S(1)} %all_to_all.30.x_ref), custom_call_target="tpu_custom_call" | custom-call | flops 4000000000 | bytes 1000000 | tf_op jit(solution)/shard_map/forward/pallas_call | solution.py:356
  70.2 4.4 %all-to-all-start.2 = ((bf16[4,112,384]{2,1,0:T(8,128)(2,1)}), bf16[4,112,384]{2,1,0:T(8,128)(2,1)S(1)}, u32[]{:S(2)}, u32[]{:S(2)}) async-start(bf16[4,112,384]{2,1,0:T(8,128)(2,1)} %get-tuple-element.30), calls=%async_computation.2 | async-start | bytes 688128 | tf_op jit(solution)/shard_map/all_to_all | solution.py:420
  74.6 10.8 %all-to-all-done.2.r_ref = bf16[4,112,384]{2,1,0:T(8,128)(2,1)S(1)} async-done(((bf16[4,112,384]{2,1,0:T(8,128)(2,1)}), bf16[4,112,384]{2,1,0:T(8,128)(2,1)S(1)}, u32[]{:S(2)}, u32[]{:S(2)}) %all-to-all-start.2) | async-done | bytes 344096 | tf_op jit(solution)/shard_map/all_to_all | solution.py:420
  85.3 1.9 %combine.1 = bf16[32,16,128]{2,1,0:T(8,128)(2,1)} custom-call(s32[1]{0:T(128)} %bitcast.y_ref, s32[32]{0:T(128)S(1)} %get-tuple-element.33.sc_ref, bf16[4,112,384]{2,1,0:T(8,128)(2,1)S(1)} %all-to-all-done.2.r_ref, bf16[1024,384]{1,0:T(8,128)(2,1)S(1)} %all_gather.3.grad_ref, f32[8,384]{1,0:T(8,128)S(1)} %get-tuple-element.29.spot_ref), custom_call_target="tpu_custom_call" | custom-call | flops 100000000 | bytes 1000000 | tf_op jit(solution)/shard_map/combine/pallas_call | solution.py:356
  87.3 4.3 %all-to-all-start.3 = ((bf16[32,16,128]{2,1,0:T(8,128)(2,1)}), bf16[32,16,128]{2,1,0:T(8,128)(2,1)S(1)}, u32[]{:S(2)}, u32[]{:S(2)}) async-start(bf16[32,16,128]{2,1,0:T(8,128)(2,1)} %combine.1), calls=%async_computation.3 | async-start | bytes 262144 | tf_op jit(solution)/shard_map/all_to_all | solution.py:420
  91.6 10.4 %backward.1 = (bf16[4,192,128]{2,1,0:T(8,128)(2,1)S(1)}, bf16[8,400,128]{2,1,0:T(8,128)(2,1)S(1)}, s32[32]{0:T(128)}) custom-call(bf16[8,400,128]{2,1,0:T(8,128)(2,1)S(1)} %all-to-all-done._.kv_ref, bf16[4,144,384]{2,1,0:T(8,128)(2,1)S(1)} %all_to_all.30.x_ref, bf16[4,112,384]{2,1,0:T(8,128)(2,1)S(1)} %all-to-all-done.2.r_ref), custom_call_target="tpu_custom_call" | custom-call | flops 8000000000 | bytes 1000000 | tf_op jit(solution)/shard_map/backward/pallas_call | solution.py:356
  102.0 2.2 %all-to-all-done.3 = bf16[32,16,128]{2,1,0:T(8,128)(2,1)S(1)} async-done(((bf16[32,16,128]{2,1,0:T(8,128)(2,1)}), bf16[32,16,128]{2,1,0:T(8,128)(2,1)S(1)}, u32[]{:S(2)}, u32[]{:S(2)}) %all-to-all-start.3) | async-done | bytes 131104 | tf_op jit(solution)/shard_map/all_to_all | solution.py:420
  104.2 23.8 %all_to_all.31.got_ref = bf16[8,400,128]{2,1,0:T(8,128)(2,1)S(1)} all-to-all(bf16[8,400,128]{2,1,0:T(8,128)(2,1)S(1)} %broadcast_dynamic-update-slice_fusion), channel_id=1, replica_groups={{0,16,32,48,64,80,96,112},{128,144,160,176,192,208,224,240},{256,272,28..., dimensions={0} | all-to-all | bytes 1638400 | tf_op jit(solution)/shard_map/all_to_all | solution.py:420
  128.1 0.7 pad_maximum_fusion
  128.8 5.1 %all-to-all-start.5 = ((bf16[4,320,128]{2,1,0:T(8,128)(2,1)}), bf16[4,320,128]{2,1,0:T(8,128)(2,1)S(1)}, u32[]{:S(2)}, u32[]{:S(2)}) async-start(bf16[4,320,128]{2,1,0:T(8,128)(2,1)} %pad_maximum_fusion), calls=%async_computation.5 | async-start | bytes 655360 | tf_op jit(solution)/shard_map/all_to_all | solution.py:420
  133.9 0.9 keys_out.1
  134.8 9.1 %all-to-all-done.5.got_ref = bf16[4,320,128]{2,1,0:T(8,128)(2,1)S(1)} async-done(((bf16[4,320,128]{2,1,0:T(8,128)(2,1)}), bf16[4,320,128]{2,1,0:T(8,128)(2,1)S(1)}, u32[]{:S(2)}, u32[]{:S(2)}) %all-to-all-start.5) | async-done | bytes 327712 | tf_op jit(solution)/shard_map/all_to_all | solution.py:420
  143.9 0.8 rest_out.1
  (4 shorter events, 0.1 us)
Async XLA Ops:
  2.0 0.8 copy-start.2
  2.8 0.8 copy-start.3
  3.6 0.8 copy-start.4
  5.6 34.1 %all-to-all-start = ((bf16[8,400,128]{2,1,0:T(8,128)(2,1)}), bf16[8,400,128]{2,1,0:T(8,128)(2,1)S(1)}, u32[]{:S(2)}, u32[]{:S(2)}) async-start(bf16[8,400,128]{2,1,0:T(8,128)(2,1)} %get-tuple-element.27), calls=%async_computation | async-start | bytes 1638400 | tf_op jit(solution)/shard_map/all_to_all | solution.py:420
  15.9 23.8 %copy-start = (bf16[64,1024]{1,0:T(8,128)(2,1)S(1)}, bf16[64,1024]{1,0:T(8,128)(2,1)}, u32[]{:S(2)}) copy-start(bf16[64,1024]{1,0:T(8,128)(2,1)} %w_ref.1) | copy-start | bytes 393220
  15.9 23.8 %copy-start.1 = (bf16[64,384]{1,0:T(8,128)(2,1)S(1)}, bf16[64,384]{1,0:T(8,128)(2,1)}, u32[]{:S(2)}) copy-start(bf16[64,384]{1,0:T(8,128)(2,1)} %queries_ref.1) | copy-start | bytes 147460
  70.2 15.1 %all-to-all-start.2 = ((bf16[4,112,384]{2,1,0:T(8,128)(2,1)}), bf16[4,112,384]{2,1,0:T(8,128)(2,1)S(1)}, u32[]{:S(2)}, u32[]{:S(2)}) async-start(bf16[4,112,384]{2,1,0:T(8,128)(2,1)} %get-tuple-element.30), calls=%async_computation.2 | async-start | bytes 688128 | tf_op jit(solution)/shard_map/all_to_all | solution.py:420
  87.3 16.9 %all-to-all-start.3 = ((bf16[32,16,128]{2,1,0:T(8,128)(2,1)}), bf16[32,16,128]{2,1,0:T(8,128)(2,1)S(1)}, u32[]{:S(2)}, u32[]{:S(2)}) async-start(bf16[32,16,128]{2,1,0:T(8,128)(2,1)} %combine.1), calls=%async_computation.3 | async-start | bytes 262144 | tf_op jit(solution)/shard_map/all_to_all | solution.py:420
  128.8 15.1 %all-to-all-start.5 = ((bf16[4,320,128]{2,1,0:T(8,128)(2,1)}), bf16[4,320,128]{2,1,0:T(8,128)(2,1)S(1)}, u32[]{:S(2)}, u32[]{:S(2)}) async-start(bf16[4,320,128]{2,1,0:T(8,128)(2,1)} %pad_maximum_fusion), calls=%async_computation.5 | async-start | bytes 655360 | tf_op jit(solution)/shard_map/all_to_all | solution.py:420

commit v3 on v2

--- a/solution.py
+++ b/solution.py
@@ -66,15 +66,29 @@
     return jnp.where(iota((TB, TB), 0).astype(F32) == spot, 1.0, 0.0).astype(BF)
 
 
-def prepare_kernel(count_ref, keys_ref, values_ref, out_grad_ref, keep_ref, kv_ref, grad_ref, spot_ref):
+def prepare_kernel(
+    count_ref, keys_ref, values_ref, out_grad_ref, keep_ref, kv_ref, grad_ref, spot_ref, both_ref, held_ref, kept_ref, sems
+):
+    loads = [
+        pltpu.make_async_copy(keep_ref, kept_ref, sems.at[0]),
+        pltpu.make_async_copy(out_grad_ref, held_ref, sems.at[1]),
+        pltpu.make_async_copy(keys_ref, both_ref.at[0:HD], sems.at[2]),
+        pltpu.make_async_copy(values_ref, both_ref.at[HD : 2 * HD], sems.at[3]),
+    ]
+    for load in loads:
+        load.start()
     count = count_ref[0]
-    live = jnp.where(iota((8, TB), 1) < count, keep_ref[...].astype(F32), 0.0)
-    grad_ref[...] = out_grad_ref[...] * live[0:1].astype(BF)
     upto = jnp.where(iota((TB, TB), 0) <= iota((TB, TB), 1), 1.0, 0.0).astype(BF)
+    loads[0].wait()
+    keep = jnp.broadcast_to(kept_ref[...].astype(F32)[None, :], (8, TB))
+    live = jnp.where(iota((8, TB), 1) < count, keep, 0.0)
     order = dot(live.astype(BF), upto)
     spot_ref[...] = jnp.where(live > 0.0, order - 1.0, -1.0)
-    both = jnp.concatenate([keys_ref[...], values_ref[...]], 0)
-    turned = dot_nt(eye(TB), both).astype(BF)
+    loads[1].wait()
+    grad_ref[...] = held_ref[...] * live[0:1].astype(BF)
+    loads[2].wait()
+    loads[3].wait()
+    turned = dot_nt(eye(TB), both_ref[...]).astype(BF)
     high = (count // 16).astype(F32)
     low = (count % 16).astype(F32)
     meta = two_rows((EXT, CH), high, low)
@@ -247,9 +261,9 @@
         attn = attn + r_ref[s, 0:HD, :].astype(F32) * share[s : s + 1]
     attn = dot(attn.astype(BF), place_matrix(spot_ref[0:1, :])).astype(BF)
     for z in range(NZ):
-        part = dot_nt(attn, grad_ref[z * CH : (z + 1) * CH, :])
+        part = dot_nt(attn, grad_ref[z * CH : (z + 1) * CH, :]).astype(BF)
         for y in range(NY):
-            out_ref[y * NZ + z] = part[y * 16 : (y + 1) * 16, :].astype(BF)
+            out_ref[y * NZ + z] = part
 
 
 def backward_kernel(
@@ -309,40 +323,34 @@
     for b in range(NY):
         start, shift = lane_window(sc_ref[QUERY_AT + b])
         part = unpack_lanes(dqa_ref[:, pl.ds(start, WIDE)], shift, sc_ref[QUERY_SIZE + b])
-        part = (0.125 * part).astype(BF)
         for c in range(NCH):
-            dq_ref[b, c * HD : (c + 1) * HD, :] = part[:, c * CH : (c + 1) * CH]
+            dq_ref[b, c * HD : (c + 1) * HD, :] = (0.125 * part[:, c * CH : (c + 1) * CH]).astype(BF)
     krow = iota((TB, CH), 0)
     for b in range(NZ):
         got = dkva_ref[pl.ds(pl.multiple_of(sc_ref[KEY_AT + b], 16), TB), :]
         dkv_ref[b, 0:TB, :] = jnp.where(krow < sc_ref[KEY_SIZE + b], got, 0.0).astype(BF)
-        dkv_ref[b, TB : TB + EXT, :] = jnp.zeros((EXT, CH), BF)
-
-
-def keys_out_kernel(got_ref, dk_ref, dv_ref):
+        dkv_ref[b, TB : TB + HD, :] = jnp.zeros((HD, CH), BF)
+
+
+def finish_kernel(y_ref, got_ref, dq_in_ref, spot_ref, dq_ref, dk_ref, dv_ref, dw_ref):
     total = got_ref[0, 0:TB, :].astype(F32)
     for z in range(1, NZ):
         total = total + got_ref[z, 0:TB, :].astype(F32)
     turned = dot_nt(eye(CH), total.astype(BF)).astype(BF)
     dk_ref[...] = turned[0:HD]
     dv_ref[...] = turned[HD:]
-
-
-def rest_out_kernel(got_ref, spot_ref, dq_ref, dw_ref):
+    for z in range(NZ):
+        dw_ref[:, z * CH : (z + 1) * CH] = got_ref[z, TB : TB + HD, :].astype(F32)
     place = place_matrix(spot_ref[0:1, :])
-    total = got_ref[0, 0 : NCH * HD, :].astype(F32)
+    own = y_ref[0]
+    dq_sum = dq_in_ref[0, own].astype(F32)
     for y in range(1, NY):
-        total = total + got_ref[y, 0 : NCH * HD, :].astype(F32)
-    total = total.astype(BF)
-    dq = dot(total[0:HD], place[0:CH])
+        dq_sum = dq_sum + dq_in_ref[y, own].astype(F32)
+    dq_sum = dq_sum.astype(BF)
+    dq = dot(dq_sum[0:HD], place[0:CH])
     for c in range(1, NCH):
-        dq = dq + dot(total[c * HD : (c + 1) * HD], place[c * CH : (c + 1) * CH])
+        dq = dq + dot(dq_sum[c * HD : (c + 1) * HD], place[c * CH : (c + 1) * CH])
     dq_ref[...] = dq.astype(BF)
-    base = NCH * HD
-    for y in range(NY):
-        for z in range(NZ):
-            part = got_ref[y, base + z * 16 : base + (z + 1) * 16, :]
-            dw_ref[y * 16 : (y + 1) * 16, z * CH : (z + 1) * CH] = part.astype(F32)
 
 
 VMEM = pl.BlockSpec(memory_space=pltpu.VMEM)
@@ -358,7 +366,7 @@
         out_shape=tuple(jax.ShapeDtypeStruct(s, d) for s, d in outs),
         in_specs=ins,
         out_specs=tuple(out_spaces),
-        scratch_shapes=[pltpu.VMEM(s, d) for s, d in scratch],
+        scratch_shapes=[pltpu.VMEM(*item) if isinstance(item, tuple) else item for item in scratch],
         compiler_params=pltpu.CompilerParams(vmem_limit_bytes=limit * MIB),
         cost_estimate=pl.CostEstimate(flops=flops, bytes_accessed=10**6, transcendentals=0),
         name=name,
@@ -367,8 +375,9 @@
 
 def prepare(count, keys, values, out_grad, keep):
     outs = [((NZ, TB + EXT, CH), BF), ((HD, TB), BF), ((8, TB), F32)]
+    scratch = [((2 * HD, TB), BF), ((HD, TB), BF), ((TB,), jnp.int32), pltpu.SemaphoreType.DMA((4,))]
     args = (count, keys, values, out_grad, keep)
-    return call(prepare_kernel, "prepare", outs, [SMEM] + [BLOCK] * 3 + [VMEM], [VMEM] * 3, [], 10**8, args)
+    return call(prepare_kernel, "prepare", outs, [SMEM] + [ANY] * 4, [VMEM] * 3, scratch, 10**8, args, 56)
 
 
 def project(w_out, grad_all, queries, spot, after):
@@ -388,13 +397,13 @@
 
 
 def combine(own, sc, got, grad_all, spot):
-    outs = [((NY * NZ, 16, CH), BF)]
+    outs = [((NY * NZ, HD, CH), BF)]
     args = (own, sc, got, grad_all, spot)
     return call(combine_kernel, "combine", outs, [SMEM] * 2 + [VMEM] * 3, [VMEM], [((8, QPAD), F32)], 10**8, args)[0]
 
 
 def backward(kv_all, x_all, got):
-    outs = [((NY, NCH * HD, CH), BF), ((NZ, TB + EXT, CH), BF), ((32,), jnp.int32)]
+    outs = [((NY, NCH * HD, CH), BF), ((NZ, TB + HD, CH), BF), ((32,), jnp.int32)]
     scratch = PACKED + [
         ((2 * CH, QPAD), BF),
         ((QPAD, CH), BF),
@@ -406,14 +415,10 @@
     return call(backward_kernel, "backward", outs, [VMEM] * 3, [VMEM] * 2 + [SMEM], scratch, 8 * 10**9, args, 20)
 
 
-def keys_out(got):
-    outs = [((HD, TB), BF), ((HD, TB), BF)]
-    return call(keys_out_kernel, "keys_out", outs, [VMEM], [VMEM] * 2, [], 10**7, (got,))
-
-
-def rest_out(got, spot):
-    outs = [((HD, TB), BF), ((HD, D), F32)]
-    return call(rest_out_kernel, "rest_out", outs, [VMEM] * 2, [VMEM] * 2, [], 10**7, (got, spot))
+def finish(got, dq_all, spot, own):
+    outs = [((HD, TB), BF), ((HD, TB), BF), ((HD, TB), BF), ((HD, D), F32)]
+    args = (own, got, dq_all, spot)
+    return call(finish_kernel, "finish", outs, [SMEM] + [VMEM] * 3, [VMEM] * 4, [], 10**7, args)
 
 
 def exchange(slots, axis, groups=None):
@@ -421,7 +426,7 @@
 
 
 def on_device(queries, keys, values, out_grad, w_out, counts, keep):
-    kv, grad, spot = prepare(counts, keys, values, out_grad, keep.reshape(1, TB))
+    kv, grad, spot = prepare(counts, keys, values, out_grad, keep)
     kv_all = exchange(kv, "tok", Z_GROUPS)
     grad_all = lax.all_gather(grad, "head", axis=0, tiled=True)
     x_all = exchange(project(w_out, grad_all, queries, spot, kv_all), "tok", Y_GROUPS)
@@ -430,15 +435,10 @@
     own = (lax.axis_index("tok") // NZ).astype(jnp.int32).reshape(1)
     parts = exchange(combine(own, sc, got, grad_all, spot), "tok")
     dq_parts, dkv_parts, _ = backward(kv_all, x_all, got)
+    dq_all = lax.all_gather(dq_parts, "tok", axis=0, axis_index_groups=Y_GROUPS)
     piece = jnp.sum(parts.astype(F32), axis=0).astype(BF)
     dkv_parts = dkv_parts.at[:, TB:, :].set(piece[None])
-    dkv_got = exchange(dkv_parts, "tok", Z_GROUPS)
-    row_pieces = dkv_got[:, TB:, :].reshape(1, NZ * 16, CH)
-    last = jnp.concatenate([dq_parts, jnp.broadcast_to(row_pieces, (NY, NZ * 16, CH))], 1)
-    last = exchange(last, "tok", Y_GROUPS)
-    dk, dv = keys_out(dkv_got)
-    dq, d_wout = rest_out(last, spot)
-    return dq, dk, dv, d_wout
+    return finish(exchange(dkv_parts, "tok", Z_GROUPS), dq_all, spot, own)
 
 
 def solution(mesh):

time: 145 us -> 138 us (0.952)
  the two profiles are of different devices: /device:TPU:6 before, /device:TPU:32 now
where the time goes in v3:
time: 138 us; the launch traced here: 136 us
  blocking collectives  57.2 us (41%)
  starting transfers between devices  34.4 us (25%)
  waiting for transfers between devices  23.7 us (17%)
  Pallas kernels  18.7 us (14%)
    all_to_all x4, starting transfers between devices, exchange(): lax.all_to_all(slots, axis, 0, 0, tiled=True, axis_index_groups=groups)  34.4 us
    all_to_all x4, waiting for transfers between devices, exchange(): lax.all_to_all(slots, axis, 0, 0, tiled=True, axis_index_groups=groups)  23.7 us
    all_gather x1, blocking collectives, on_device(): grad_all = lax.all_gather(grad, 'head', axis=0, tiled=True)  22.6 us
    pallas_call x6, Pallas kernels, call(): pl.pallas_call(kernel, out_shape=tuple((jax.ShapeDtypeStruct(s, d) for s,...  18.7 us
    all_to_all x1, blocking collectives, exchange(): lax.all_to_all(slots, axis, 0, 0, tiled=True, axis_index_groups=groups)  17.3 us
    all_gather x1, blocking collectives, on_device(): dq_all = lax.all_gather(dq_parts, 'tok', axis=0, axis_index_groups=Y_GROUPS)  17.3 us
  transfers between devices with their start and end apart: 4, of which 4 were waited for; matrix products, arithmetic and copies ran while one was open for 0% of the time, Pallas kernels for 5%

profile of v3, /device:TPU:32, one launch (start us, length us, event | category | flops | bytes accessed | tf_op | source)
XLA Modules:
  0.0 136.2 jit_solution(5527157643185622349)
XLA Ops:
  1.3 2.1 %prepare.1 = (bf16[8,400,128]{2,1,0:T(8,128)(2,1)}, bf16[64,384]{1,0:T(8,128)(2,1)}, f32[8,384]{1,0:T(8,128)}) custom-call(s32[1]{0:T(128)S(6)} %copy.12.count_ref, bf16[64,384]{1,0:T(8,128)(2,1)} %keys_ref.1, bf16[64,384]{1,0:T(8,128)(2,1)} %values_ref.1, bf16[64,384]{1,0:T(8,128)(2,1)} %out_grad_ref.1, s32[384]{0:T(512)} %keep_ref.1), custom_call_target="tpu_custom_call" | custom-call | flops 100000000 | bytes 1000000 | tf_op jit(solution)/shard_map/prepare/pallas_call | solution.py:364
  3.4 0.0 copy-start.3
  3.4 10.5 %all-to-all-start = ((bf16[8,400,128]{2,1,0:T(8,128)(2,1)}), bf16[8,400,128]{2,1,0:T(8,128)(2,1)S(1)}, u32[]{:S(2)}, u32[]{:S(2)}) async-start(bf16[8,400,128]{2,1,0:T(8,128)(2,1)} %get-tuple-element.23), calls=%async_computation | async-start | bytes 1638400 | tf_op jit(solution)/shard_map/all_to_all | solution.py:425
  13.9 0.0 copy-done.3
  13.9 0.0 copy-start
  13.9 0.0 copy-start.1
  13.9 0.0 copy-start.2
  13.9 22.6 %all_gather.9.grad_ref = bf16[1024,384]{1,0:T(8,128)(2,1)S(1)} all-gather(bf16[64,384]{1,0:T(8,128)(2,1)S(1)} %copy-done.3), channel_id=1, replica_groups=mesh['tok'=32,'head'=16] {'head'}, dimensions={0}, use_global_device_ids=true | all-gather | bytes 835584 | tf_op jit(solution)/shard_map/all_gather | solution.py:431
  36.5 1.1 all-to-all-done._.kv_ref
  37.7 0.0 copy-done
  37.7 0.0 copy-done.1
  37.7 0.0 copy-done.2
  37.7 0.4 project.1
  38.1 17.3 %all_to_all.25.x_ref = bf16[4,144,384]{2,1,0:T(8,128)(2,1)S(1)} all-to-all(bf16[4,144,384]{2,1,0:T(8,128)(2,1)S(1)} %project.1), channel_id=1, replica_groups={{0,128,256,384},{16,144,272,400},{32,160,288,416},{48,176,304,432},{64,..., dimensions={0} | all-to-all | bytes 884736 | tf_op jit(solution)/shard_map/all_to_all | solution.py:425
  55.5 5.6 %forward.1 = (bf16[4,112,384]{2,1,0:T(8,128)(2,1)}, s32[32]{0:T(128)S(1)}) custom-call(bf16[8,400,128]{2,1,0:T(8,128)(2,1)S(1)} %all-to-all-done._.kv_ref, bf16[4,144,384]{2,1,0:T(8,128)(2,1)S(1)} %all_to_all.25.x_ref), custom_call_target="tpu_custom_call" | custom-call | flops 4000000000 | bytes 1000000 | tf_op jit(solution)/shard_map/forward/pallas_call | solution.py:364
  61.1 7.8 %all-to-all-start.2 = ((bf16[4,112,384]{2,1,0:T(8,128)(2,1)}), bf16[4,112,384]{2,1,0:T(8,128)(2,1)S(1)}, u32[]{:S(2)}, u32[]{:S(2)}) async-start(bf16[4,112,384]{2,1,0:T(8,128)(2,1)} %get-tuple-element.26), calls=%async_computation.2 | async-start | bytes 688128 | tf_op jit(solution)/shard_map/all_to_all | solution.py:425
  68.9 5.9 %all-to-all-done.2.r_ref = bf16[4,112,384]{2,1,0:T(8,128)(2,1)S(1)} async-done(((bf16[4,112,384]{2,1,0:T(8,128)(2,1)}), bf16[4,112,384]{2,1,0:T(8,128)(2,1)S(1)}, u32[]{:S(2)}, u32[]{:S(2)}) %all-to-all-start.2) | async-done | bytes 344096 | tf_op jit(solution)/shard_map/all_to_all | solution.py:425
  74.8 2.1 %combine.1 = bf16[32,64,128]{2,1,0:T(8,128)(2,1)} custom-call(s32[1]{0:T(128)} %bitcast.y_ref, s32[32]{0:T(128)S(1)} %get-tuple-element.28.sc_ref, bf16[4,112,384]{2,1,0:T(8,128)(2,1)S(1)} %all-to-all-done.2.r_ref, bf16[1024,384]{1,0:T(8,128)(2,1)S(1)} %all_gather.9.grad_ref, f32[8,384]{1,0:T(8,128)S(1)} %copy-done.1), custom_call_target="tpu_custom_call" | custom-call | flops 100000000 | bytes 1000000 | tf_op jit(solution)/shard_map/combine/pallas_call | solution.py:364
  76.9 12.2 %all-to-all-start.3 = ((bf16[32,64,128]{2,1,0:T(8,128)(2,1)}), bf16[32,64,128]{2,1,0:T(8,128)(2,1)S(1)}, u32[]{:S(2)}, u32[]{:S(2)}) async-start(bf16[32,64,128]{2,1,0:T(8,128)(2,1)} %combine.1), calls=%async_computation.3 | async-start | bytes 1048576 | tf_op jit(solution)/shard_map/all_to_all | solution.py:425
  89.1 7.5 %backward.1 = (bf16[4,192,128]{2,1,0:T(8,128)(2,1)S(1)}, bf16[8,448,128]{2,1,0:T(8,128)(2,1)}, s32[32]{0:T(128)}) custom-call(bf16[8,400,128]{2,1,0:T(8,128)(2,1)S(1)} %all-to-all-done._.kv_ref, bf16[4,144,384]{2,1,0:T(8,128)(2,1)S(1)} %all_to_all.25.x_ref, bf16[4,112,384]{2,1,0:T(8,128)(2,1)S(1)} %all-to-all-done.2.r_ref), custom_call_target="tpu_custom_call" | custom-call | flops 8000000000 | bytes 1000000 | tf_op jit(solution)/shard_map/backward/pallas_call | solution.py:364
  96.5 8.1 %all-to-all-done.3 = bf16[32,64,128]{2,1,0:T(8,128)(2,1)S(1)} async-done(((bf16[32,64,128]{2,1,0:T(8,128)(2,1)}), bf16[32,64,128]{2,1,0:T(8,128)(2,1)S(1)}, u32[]{:S(2)}, u32[]{:S(2)}) %all-to-all-start.3) | async-done | bytes 524320 | tf_op jit(solution)/shard_map/all_to_all | solution.py:425
  104.7 0.1 reduce_sum.12
  104.8 0.7 broadcast_dynamic-update-slice_fusion
  105.5 4.0 %all-to-all-start.4 = ((bf16[8,448,128]{2,1,0:T(8,128)(2,1)}), bf16[8,448,128]{2,1,0:T(8,128)(2,1)S(1)}, u32[]{:S(2)}, u32[]{:S(2)}) async-start(bf16[8,448,128]{2,1,0:T(8,128)(2,1)} %broadcast_dynamic-update-slice_fusion), calls=%async_computation.4 | async-start | bytes 1835008 | tf_op jit(solution)/shard_map/all_to_all | solution.py:425
  109.4 17.3 %all-gather = bf16[16,192,128]{2,1,0:T(8,128)(2,1)S(1)} all-gather(bf16[4,192,128]{2,1,0:T(8,128)(2,1)S(1)} %get-tuple-element.29), channel_id=2, replica_groups={{0,128,256,384},{16,144,272,400},{32,160,288,416},{48,176,304,432},{64,..., dimensions={0}, use_global_device_ids=true | all-gather | bytes 983040 | tf_op jit(solution)/shard_map/all_gather | solution.py:438
  126.7 8.5 %all-to-all-done.4.got_ref = bf16[8,448,128]{2,1,0:T(8,128)(2,1)S(1)} async-done(((bf16[8,448,128]{2,1,0:T(8,128)(2,1)}), bf16[8,448,128]{2,1,0:T(8,128)(2,1)S(1)}, u32[]{:S(2)}, u32[]{:S(2)}) %all-to-all-start.4) | async-done | bytes 917536 | tf_op jit(solution)/shard_map/all_to_all | solution.py:425
  135.2 1.0 finish.1
Async XLA Ops:
  3.4 10.5 %copy-start.3 = (bf16[64,384]{1,0:T(8,128)(2,1)S(1)}, bf16[64,384]{1,0:T(8,128)(2,1)}, u32[]{:S(2)}) copy-start(bf16[64,384]{1,0:T(8,128)(2,1)} %get-tuple-element.24) | copy-start | bytes 147460
  3.4 34.3 %all-to-all-start = ((bf16[8,400,128]{2,1,0:T(8,128)(2,1)}), bf16[8,400,128]{2,1,0:T(8,128)(2,1)S(1)}, u32[]{:S(2)}, u32[]{:S(2)}) async-start(bf16[8,400,128]{2,1,0:T(8,128)(2,1)} %get-tuple-element.23), calls=%async_computation | async-start | bytes 1638400 | tf_op jit(solution)/shard_map/all_to_all | solution.py:425
  13.9 23.8 %copy-start = (bf16[64,1024]{1,0:T(8,128)(2,1)S(1)}, bf16[64,1024]{1,0:T(8,128)(2,1)}, u32[]{:S(2)}) copy-start(bf16[64,1024]{1,0:T(8,128)(2,1)} %w_ref.1) | copy-start | bytes 393220
  13.9 23.8 %copy-start.1 = (f32[8,384]{1,0:T(8,128)S(1)}, f32[8,384]{1,0:T(8,128)}, u32[]{:S(2)}) copy-start(f32[8,384]{1,0:T(8,128)} %get-tuple-element.25.spot_ref) | copy-start | bytes 36868
  13.9 23.8 %copy-start.2 = (bf16[64,384]{1,0:T(8,128)(2,1)S(1)}, bf16[64,384]{1,0:T(8,128)(2,1)}, u32[]{:S(2)}) copy-start(bf16[64,384]{1,0:T(8,128)(2,1)} %queries_ref.1) | copy-start | bytes 147460
  61.1 13.7 %all-to-all-start.2 = ((bf16[4,112,384]{2,1,0:T(8,128)(2,1)}), bf16[4,112,384]{2,1,0:T(8,128)(2,1)S(1)}, u32[]{:S(2)}, u32[]{:S(2)}) async-start(bf16[4,112,384]{2,1,0:T(8,128)(2,1)} %get-tuple-element.26), calls=%async_computation.2 | async-start | bytes 688128 | tf_op jit(solution)/shard_map/all_to_all | solution.py:425
  76.9 27.8 %all-to-all-start.3 = ((bf16[32,64,128]{2,1,0:T(8,128)(2,1)}), bf16[32,64,128]{2,1,0:T(8,128)(2,1)S(1)}, u32[]{:S(2)}, u32[]{:S(2)}) async-start(bf16[32,64,128]{2,1,0:T(8,128)(2,1)} %combine.1), calls=%async_computation.3 | async-start | bytes 1048576 | tf_op jit(solution)/shard_map/all_to_all | solution.py:425
  105.5 29.8 %all-to-all-start.4 = ((bf16[8,448,128]{2,1,0:T(8,128)(2,1)}), bf16[8,448,128]{2,1,0:T(8,128)(2,1)S(1)}, u32[]{:S(2)}, u32[]{:S(2)}) async-start(bf16[8,448,128]{2,1,0:T(8,128)(2,1)} %broadcast_dynamic-update-slice_fusion), calls=%async_computation.4 | async-start | bytes 1835008 | tf_op jit(solution)/shard_map/all_to_all | solution.py:425

commit v4 on v3

--- a/solution.py
+++ b/solution.py
@@ -189,7 +189,7 @@
     ws_ref[...] = jnp.zeros(ws_ref.shape, BF)
     ws_ref[0:HD, :] = xp_ref[0:HD, :].astype(BF)
     ws_ref[CH : CH + EXT, :] = jnp.where(iota((EXT, QPAD), 0) == 0, 1.0, 0.0).astype(BF)
-    st_ref[...] = jnp.where(iota((8, QPAD), 0) == 1, 1.0, 0.0)
+    st_ref[...] = jnp.zeros(st_ref.shape, F32)
     acc_ref[...] = jnp.zeros(acc_ref.shape, F32)
 
     def query_tile(qt, _):
@@ -210,41 +210,40 @@
         total = acc[HD : HD + 1]
         dsum = jnp.sum(acc[0:HD] * xp_ref[HD : 2 * HD, pl.ds(q0, TQ)], axis=0, keepdims=True)
         acc_ref[:, pl.ds(q0, TQ)] = acc[0:HD] / total
-        st_ref[0:1, pl.ds(q0, TQ)] = top
-        st_ref[1:2, pl.ds(q0, TQ)] = total
-        st_ref[2:3, pl.ds(q0, TQ)] = dsum
+        st_ref[0:1, pl.ds(q0, TQ)] = top + jnp.log(total)
+        st_ref[1:2, pl.ds(q0, TQ)] = dsum / total
         return 0
 
     lax.fori_loop(0, n_query_tiles, query_tile, 0)
 
-    rows = [st_ref[i : i + 1, q * TB : (q + 1) * TB] for i in range(3) for q in range(NY)]
-    split = pieces(jnp.concatenate(rows + [jnp.zeros((4, TB), F32)], 0))
+    rows = [st_ref[i : i + 1, q * TB : (q + 1) * TB] for i in range(2) for q in range(NY)]
+    split = [piece.astype(F32) for piece in pieces(jnp.concatenate(rows, 0))]
+    stats = jnp.concatenate(split + [jnp.zeros((8, TB), F32)], 0).astype(BF)
     for b in range(NY):
         start, shift = lane_window(sc_ref[QUERY_AT + b])
         part = unpack_lanes(acc_ref[:, pl.ds(start, WIDE)], shift, sc_ref[QUERY_SIZE + b])
         out_ref[b, 0:HD, :] = part.astype(BF)
-        for i in range(3):
-            out_ref[b, HD + i * EXT : HD + (i + 1) * EXT, :] = split[i]
+        out_ref[b, HD : HD + 2 * EXT, :] = stats
 
 
 def merged_stats(r_ref):
-    stats = []
+    lses = []
+    deltas = []
     for s in range(NY):
-        st = r_ref[s, HD : HD + EXT, :].astype(F32)
-        st = st + r_ref[s, HD + EXT : HD + 2 * EXT, :].astype(F32)
-        stats.append(st + r_ref[s, HD + 2 * EXT : HD + 3 * EXT, :].astype(F32))
-    top = stats[0][0:NY]
+        st = r_ref[s, HD : HD + 2 * EXT, :].astype(F32)
+        st = st[0:8] + st[8:16] + st[16:24]
+        lses.append(st[0:NY])
+        deltas.append(st[NY : 2 * NY])
+    top = lses[0]
     for s in range(1, NY):
-        top = jnp.maximum(top, stats[s][0:NY])
-    shares = []
-    total = jnp.zeros((NY, TB), F32)
-    dsum = jnp.zeros((NY, TB), F32)
+        top = jnp.maximum(top, lses[s])
+    weights = [jnp.exp(lse - top) for lse in lses]
+    total = weights[0] + weights[1] + weights[2] + weights[3]
+    shares = [weight / total for weight in weights]
+    delta = jnp.zeros((NY, TB), F32)
     for s in range(NY):
-        fade = jnp.exp(stats[s][0:NY] - top)
-        shares.append(stats[s][NY : 2 * NY] * fade)
-        total = total + shares[s]
-        dsum = dsum + stats[s][2 * NY : 3 * NY] * fade
-    return top + jnp.log(total), dsum / total, [share / total for share in shares]
+        delta = delta + shares[s] * deltas[s]
+    return top + jnp.log(total), delta, shares
 
 
 def combine_kernel(y_ref, sc_ref, r_ref, grad_ref, spot_ref, out_ref, share_ref):
@@ -390,7 +389,7 @@
 
 
 def forward(kv_all, x_all):
-    outs = [((NY, HD + 3 * EXT, TB), BF), ((32,), jnp.int32)]
+    outs = [((NY, HD + 2 * EXT, TB), BF), ((32,), jnp.int32)]
     scratch = PACKED + [((HD, QPAD), F32), ((8, QPAD), F32)]
     args = (kv_all, x_all)
     return call(forward_kernel, "forward", outs, [VMEM] * 2, [VMEM, SMEM], scratch, 4 * 10**9, args, 20)

time: 138 us -> 137 us (level)
  the two profiles are of different devices: /device:TPU:32 before, /device:TPU:33 now
where the time goes in v4:
time: 137 us; the launch traced here: 136 us
  blocking collectives  54.2 us (40%)
  starting transfers between devices  32.9 us (24%)
  waiting for transfers between devices  27.7 us (20%)
  Pallas kernels  18.7 us (14%)
  between operations  1.37 us (1%)
    all_to_all x4, starting transfers between devices, exchange(): lax.all_to_all(slots, axis, 0, 0, tiled=True, axis_index_groups=groups)  32.9 us
    all_to_all x4, waiting for transfers between devices, exchange(): lax.all_to_all(slots, axis, 0, 0, tiled=True, axis_index_groups=groups)  27.7 us
    all_gather x1, blocking collectives, on_device(): grad_all = lax.all_gather(grad, 'head', axis=0, tiled=True)  23.4 us
    pallas_call x6, Pallas kernels, call(): pl.pallas_call(kernel, out_shape=tuple((jax.ShapeDtypeStruct(s, d) for s,...  18.7 us
    all_to_all x1, blocking collectives, exchange(): lax.all_to_all(slots, axis, 0, 0, tiled=True, axis_index_groups=groups)  17.2 us
    all_gather x1, blocking collectives, on_device(): dq_all = lax.all_gather(dq_parts, 'tok', axis=0, axis_index_groups=Y_GROUPS)  13.5 us
  transfers between devices with their start and end apart: 4, of which 4 were waited for; matrix products, arithmetic and copies ran while one was open for 0% of the time, Pallas kernels for 5%

profile of v4, /device:TPU:33, one launch (start us, length us, event | category | flops | bytes accessed | tf_op | source)
XLA Modules:
  0.0 135.6 jit_solution(10995404602785663705)
XLA Ops:
  1.3 2.1 %prepare.1 = (bf16[8,400,128]{2,1,0:T(8,128)(2,1)}, bf16[64,384]{1,0:T(8,128)(2,1)}, f32[8,384]{1,0:T(8,128)}) custom-call(s32[1]{0:T(128)S(6)} %copy.12.count_ref, bf16[64,384]{1,0:T(8,128)(2,1)} %keys_ref.1, bf16[64,384]{1,0:T(8,128)(2,1)} %values_ref.1, bf16[64,384]{1,0:T(8,128)(2,1)} %out_grad_ref.1, s32[384]{0:T(512)} %keep_ref.1), custom_call_target="tpu_custom_call" | custom-call | flops 100000000 | bytes 1000000 | tf_op jit(solution)/shard_map/prepare/pallas_call | solution.py:363
  3.4 0.0 copy-start.3
  3.4 10.2 %all-to-all-start = ((bf16[8,400,128]{2,1,0:T(8,128)(2,1)}), bf16[8,400,128]{2,1,0:T(8,128)(2,1)S(1)}, u32[]{:S(2)}, u32[]{:S(2)}) async-start(bf16[8,400,128]{2,1,0:T(8,128)(2,1)} %get-tuple-element.23), calls=%async_computation | async-start | bytes 1638400 | tf_op jit(solution)/shard_map/all_to_all | solution.py:424
  13.6 0.0 copy-done.3
  13.6 0.0 copy-start
  13.6 0.0 copy-start.1
  13.6 0.0 copy-start.2
  13.6 23.4 %all_gather.9.grad_ref = bf16[1024,384]{1,0:T(8,128)(2,1)S(1)} all-gather(bf16[64,384]{1,0:T(8,128)(2,1)S(1)} %copy-done.3), channel_id=1, replica_groups=mesh['tok'=32,'head'=16] {'head'}, dimensions={0}, use_global_device_ids=true | all-gather | bytes 835584 | tf_op jit(solution)/shard_map/all_gather | solution.py:430
  37.0 0.8 all-to-all-done._.kv_ref
  37.9 0.0 copy-done
  37.9 0.0 copy-done.1
  37.9 0.0 copy-done.2
  37.9 0.4 project.1
  38.3 17.2 %all_to_all.25.x_ref = bf16[4,144,384]{2,1,0:T(8,128)(2,1)S(1)} all-to-all(bf16[4,144,384]{2,1,0:T(8,128)(2,1)S(1)} %project.1), channel_id=1, replica_groups={{0,128,256,384},{16,144,272,400},{32,160,288,416},{48,176,304,432},{64,..., dimensions={0} | all-to-all | bytes 884736 | tf_op jit(solution)/shard_map/all_to_all | solution.py:424
  55.5 5.6 %forward.1 = (bf16[4,96,384]{2,1,0:T(8,128)(2,1)}, s32[32]{0:T(128)S(1)}) custom-call(bf16[8,400,128]{2,1,0:T(8,128)(2,1)S(1)} %all-to-all-done._.kv_ref, bf16[4,144,384]{2,1,0:T(8,128)(2,1)S(1)} %all_to_all.25.x_ref), custom_call_target="tpu_custom_call" | custom-call | flops 4000000000 | bytes 1000000 | tf_op jit(solution)/shard_map/forward/pallas_call | solution.py:363
  61.2 6.7 %all-to-all-start.2 = ((bf16[4,96,384]{2,1,0:T(8,128)(2,1)}), bf16[4,96,384]{2,1,0:T(8,128)(2,1)S(1)}, u32[]{:S(2)}, u32[]{:S(2)}) async-start(bf16[4,96,384]{2,1,0:T(8,128)(2,1)} %get-tuple-element.26), calls=%async_computation.2 | async-start | bytes 589824 | tf_op jit(solution)/shard_map/all_to_all | solution.py:424
  67.8 4.4 %all-to-all-done.2.r_ref = bf16[4,96,384]{2,1,0:T(8,128)(2,1)S(1)} async-done(((bf16[4,96,384]{2,1,0:T(8,128)(2,1)}), bf16[4,96,384]{2,1,0:T(8,128)(2,1)S(1)}, u32[]{:S(2)}, u32[]{:S(2)}) %all-to-all-start.2) | async-done | bytes 294944 | tf_op jit(solution)/shard_map/all_to_all | solution.py:424
  72.2 2.1 %combine.1 = bf16[32,64,128]{2,1,0:T(8,128)(2,1)} custom-call(s32[1]{0:T(128)} %bitcast.y_ref, s32[32]{0:T(128)S(1)} %get-tuple-element.28.sc_ref, bf16[4,96,384]{2,1,0:T(8,128)(2,1)S(1)} %all-to-all-done.2.r_ref, bf16[1024,384]{1,0:T(8,128)(2,1)S(1)} %all_gather.9.grad_ref, f32[8,384]{1,0:T(8,128)S(1)} %copy-done.1), custom_call_target="tpu_custom_call" | custom-call | flops 100000000 | bytes 1000000 | tf_op jit(solution)/shard_map/combine/pallas_call | solution.py:363
  74.3 12.5 %all-to-all-start.3 = ((bf16[32,64,128]{2,1,0:T(8,128)(2,1)}), bf16[32,64,128]{2,1,0:T(8,128)(2,1)S(1)}, u32[]{:S(2)}, u32[]{:S(2)}) async-start(bf16[32,64,128]{2,1,0:T(8,128)(2,1)} %combine.1), calls=%async_computation.3 | async-start | bytes 1048576 | tf_op jit(solution)/shard_map/all_to_all | solution.py:424
  86.8 7.4 %backward.1 = (bf16[4,192,128]{2,1,0:T(8,128)(2,1)S(1)}, bf16[8,448,128]{2,1,0:T(8,128)(2,1)}, s32[32]{0:T(128)}) custom-call(bf16[8,400,128]{2,1,0:T(8,128)(2,1)S(1)} %all-to-all-done._.kv_ref, bf16[4,144,384]{2,1,0:T(8,128)(2,1)S(1)} %all_to_all.25.x_ref, bf16[4,96,384]{2,1,0:T(8,128)(2,1)S(1)} %all-to-all-done.2.r_ref), custom_call_target="tpu_custom_call" | custom-call | flops 8000000000 | bytes 1000000 | tf_op jit(solution)/shard_map/backward/pallas_call | solution.py:363
  94.3 9.8 %all-to-all-done.3 = bf16[32,64,128]{2,1,0:T(8,128)(2,1)S(1)} async-done(((bf16[32,64,128]{2,1,0:T(8,128)(2,1)}), bf16[32,64,128]{2,1,0:T(8,128)(2,1)S(1)}, u32[]{:S(2)}, u32[]{:S(2)}) %all-to-all-start.3) | async-done | bytes 524320 | tf_op jit(solution)/shard_map/all_to_all | solution.py:424
  104.0 0.1 reduce_sum.12
  104.1 0.7 broadcast_dynamic-update-slice_fusion
  104.8 3.6 %all-to-all-start.4 = ((bf16[8,448,128]{2,1,0:T(8,128)(2,1)}), bf16[8,448,128]{2,1,0:T(8,128)(2,1)S(1)}, u32[]{:S(2)}, u32[]{:S(2)}) async-start(bf16[8,448,128]{2,1,0:T(8,128)(2,1)} %broadcast_dynamic-update-slice_fusion), calls=%async_computation.4 | async-start | bytes 1835008 | tf_op jit(solution)/shard_map/all_to_all | solution.py:424
  108.4 13.5 %all-gather = bf16[16,192,128]{2,1,0:T(8,128)(2,1)S(1)} all-gather(bf16[4,192,128]{2,1,0:T(8,128)(2,1)S(1)} %get-tuple-element.29), channel_id=2, replica_groups={{0,128,256,384},{16,144,272,400},{32,160,288,416},{48,176,304,432},{64,..., dimensions={0}, use_global_device_ids=true | all-gather | bytes 983040 | tf_op jit(solution)/shard_map/all_gather | solution.py:437
  121.9 12.7 %all-to-all-done.4.got_ref = bf16[8,448,128]{2,1,0:T(8,128)(2,1)S(1)} async-done(((bf16[8,448,128]{2,1,0:T(8,128)(2,1)}), bf16[8,448,128]{2,1,0:T(8,128)(2,1)S(1)}, u32[]{:S(2)}, u32[]{:S(2)}) %all-to-all-start.4) | async-done | bytes 917536 | tf_op jit(solution)/shard_map/all_to_all | solution.py:424
  134.6 1.0 finish.1
Async XLA Ops:
  3.4 10.2 %copy-start.3 = (bf16[64,384]{1,0:T(8,128)(2,1)S(1)}, bf16[64,384]{1,0:T(8,128)(2,1)}, u32[]{:S(2)}) copy-start(bf16[64,384]{1,0:T(8,128)(2,1)} %get-tuple-element.24) | copy-start | bytes 147460
  3.4 34.5 %all-to-all-start = ((bf16[8,400,128]{2,1,0:T(8,128)(2,1)}), bf16[8,400,128]{2,1,0:T(8,128)(2,1)S(1)}, u32[]{:S(2)}, u32[]{:S(2)}) async-start(bf16[8,400,128]{2,1,0:T(8,128)(2,1)} %get-tuple-element.23), calls=%async_computation | async-start | bytes 1638400 | tf_op jit(solution)/shard_map/all_to_all | solution.py:424
  13.6 24.3 %copy-start = (bf16[64,1024]{1,0:T(8,128)(2,1)S(1)}, bf16[64,1024]{1,0:T(8,128)(2,1)}, u32[]{:S(2)}) copy-start(bf16[64,1024]{1,0:T(8,128)(2,1)} %w_ref.1) | copy-start | bytes 393220
  13.6 24.3 %copy-start.1 = (f32[8,384]{1,0:T(8,128)S(1)}, f32[8,384]{1,0:T(8,128)}, u32[]{:S(2)}) copy-start(f32[8,384]{1,0:T(8,128)} %get-tuple-element.25.spot_ref) | copy-start | bytes 36868
  13.6 24.3 %copy-start.2 = (bf16[64,384]{1,0:T(8,128)(2,1)S(1)}, bf16[64,384]{1,0:T(8,128)(2,1)}, u32[]{:S(2)}) copy-start(bf16[64,384]{1,0:T(8,128)(2,1)} %queries_ref.1) | copy-start | bytes 147460
  61.2 11.1 %all-to-all-start.2 = ((bf16[4,96,384]{2,1,0:T(8,128)(2,1)}), bf16[4,96,384]{2,1,0:T(8,128)(2,1)S(1)}, u32[]{:S(2)}, u32[]{:S(2)}) async-start(bf16[4,96,384]{2,1,0:T(8,128)(2,1)} %get-tuple-element.26), calls=%async_computation.2 | async-start | bytes 589824 | tf_op jit(solution)/shard_map/all_to_all | solution.py:424
  74.3 29.7 %all-to-all-start.3 = ((bf16[32,64,128]{2,1,0:T(8,128)(2,1)}), bf16[32,64,128]{2,1,0:T(8,128)(2,1)S(1)}, u32[]{:S(2)}, u32[]{:S(2)}) async-start(bf16[32,64,128]{2,1,0:T(8,128)(2,1)} %combine.1), calls=%async_computation.3 | async-start | bytes 1048576 | tf_op jit(solution)/shard_map/all_to_all | solution.py:424
  104.8 29.9 %all-to-all-start.4 = ((bf16[8,448,128]{2,1,0:T(8,128)(2,1)}), bf16[8,448,128]{2,1,0:T(8,128)(2,1)S(1)}, u32[]{:S(2)}, u32[]{:S(2)}) async-start(bf16[8,448,128]{2,1,0:T(8,128)(2,1)} %broadcast_dynamic-update-slice_fusion), calls=%async_computation.4 | async-start | bytes 1835008 | tf_op jit(solution)/shard_map/all_to_all | solution.py:424
